TPU v7x, 128 devices: a whole 4x4x4 slice. The times are simulated.
128 devices in a mesh: tex: 8 (over x, core), view: 16 (over y, z).
Axes of the slice: x: 4, y: 4, z: 4, core: 2. Of those that a mesh axis runs over, the one named last changes fastest.
Arguments:
- texel_atlas: float32 [128, 10, 4096], P(('tex', 'view'))
- observed: float32 [128, 3, 768], P('view'), may hold values from -5 to 5
- geometry: float32 [128, 6, 768], P('view'), may hold values from -1 to 1
- block_ids: int32 [128, 8, 4], P('view', 'tex'), may hold values from -1 to 15, as said below
- pixel_slot: int32 [128, 768], P('view'), may hold values from 0 to 31, as said below
- corner: int32 [128, 768], P('view'), may hold values from 0 to 3968
- bilinear_frac: float32 [128, 2, 768], P('view'), may hold values from 0 to 1
Outputs:
- update: float32 [128, 10, 4096], P(('tex', 'view'))
- solve_residual: float32 [128, 10, 4096], P(('tex', 'view'))
Inputs may be any that keep to these rules, and one draw needn't show every extreme that they name: `block_ids`: -1 marks an empty slot; for each image tile and owner the live slots come first, one to 4 of them. `pixel_slot`: always names a live slot of the pixel's own tile.
All inputs are finite; a program needn't handle non-finite values.
Results may differ from a plain program's by a relative error of at most 0.0023.
Values sent between devices are 32-bit elements; how exact they have to be, the bound alone decides.
A program may use at most 128 MiB of HBM per device.

v0:
```python
import math

import jax
import jax.numpy as jnp
from jax import lax
from jax.sharding import PartitionSpec as P

BSIDE = 64
ITERS = 2


DAMPING = 0.1


def shade(params, geometry):
    albedo = params[:, 0:3]
    specular = params[:, 3:6]
    roughness = params[:, 6]
    tilt_x = params[:, 7]
    tilt_y = params[:, 8]
    occlusion = params[:, 9]
    inverse_len = lax.rsqrt(1.0 + tilt_x * tilt_x + tilt_y * tilt_y)
    normal_x = tilt_x * inverse_len
    normal_y = tilt_y * inverse_len
    light_dir = geometry[:, 0:3]
    viewer = geometry[:, 3:6]
    halfway = light_dir + viewer
    halfway = halfway * lax.rsqrt(jnp.sum(halfway * halfway, axis=1, keepdims=True))

    def facing(vector):
        return normal_x * vector[:, 0] + normal_y * vector[:, 1] + inverse_len * vector[:, 2]

    cosine_light = facing(light_dir)
    cosine_view = facing(viewer)
    cosine_half = facing(halfway)
    view_half = jnp.sum(viewer * halfway, axis=1)
    rough_square = roughness * roughness
    rough_fourth = rough_square * rough_square
    denominator = cosine_half * cosine_half * (rough_fourth - 1.0) + 1.0
    distribution = rough_fourth / (math.pi * denominator * denominator)
    smith_k = 0.5 * rough_square
    masking = cosine_light / (cosine_light * (1.0 - smith_k) + smith_k)
    masking = masking * cosine_view / (cosine_view * (1.0 - smith_k) + smith_k)
    fresnel = specular + (1.0 - specular) * ((1.0 - view_half) ** 5)[:, None]
    reflected = (distribution * masking / (4.0 * cosine_light * cosine_view))[:, None] * fresnel
    return (occlusion * cosine_light)[:, None] * (albedo + math.pi * reflected)


def tables(slot_part, corner_part, frac_part, owner_index, slots):
    in_range = slot_part // slots == owner_index
    slot_within = slot_part % slots
    row_start = corner_part // (BSIDE - 1)
    column_start = corner_part % (BSIDE - 1)
    across = frac_part[:, 0]
    frac_down = frac_part[:, 1]
    positions = jnp.arange(BSIDE, dtype=jnp.int32)[None, :, None]
    column_weight = jnp.where(positions == column_start[:, None], (1.0 - across)[:, None], 0.0)
    column_weight = column_weight + jnp.where(
        positions == column_start[:, None] + 1, across[:, None], 0.0
    )
    row_part = jnp.where(positions == row_start[:, None], (1.0 - frac_down)[:, None], 0.0)
    row_part = row_part + jnp.where(positions == row_start[:, None] + 1, frac_down[:, None], 0.0)
    picked = (jnp.arange(slots, dtype=jnp.int32)[None, :, None] == slot_within[:, None]) & in_range[
        :, None
    ]
    row_weight = jnp.where(picked[:, :, None], row_part[:, None], 0.0)
    return (row_weight, column_weight)


def per_device(texel_atlas, observed, geometry, block_ids, pixel_slot, corner, bilinear_frac):
    tex_count = lax.axis_size("tex")
    owner_index = lax.axis_index("tex")
    own_blocks, channels, texels = texel_atlas.shape
    tiles_all = observed.shape[0]
    tiles_own = tiles_all // tex_count
    slots = block_ids.shape[2]
    groups = tiles_all // tex_count
    slot_blocks = block_ids[:, 0, :]
    slot_list = slot_blocks.reshape(-1)
    exact_mode = lax.Precision.HIGHEST

    def grouped(source):
        return source.reshape((groups, tex_count) + source.shape[1:])

    pixel_tables = (grouped(pixel_slot), grouped(corner), grouped(bilinear_frac))

    def widen(own_shard):
        return lax.all_gather(own_shard, "view", axis=0, tiled=True)

    def pixels_of(whole_range):
        fetched = jnp.take(whole_range, jnp.clip(slot_blocks, 0, whole_range.shape[0] - 1), axis=0)

        def pixels_one_group(members):
            blocks, slot_part, corner_part, frac_part = members
            row_weight, column_weight = tables(
                slot_part, corner_part, frac_part, owner_index, slots
            )
            values = blocks.reshape(blocks.shape[0], slots, channels, BSIDE, BSIDE)
            middle = jnp.einsum("tjcyx,tjyp->tcxp", values, row_weight, precision=exact_mode)
            return jnp.sum(middle * column_weight[:, None], axis=2)

        partial_value = lax.map(pixels_one_group, (grouped(fetched),) + pixel_tables)
        partial_value = partial_value.reshape((tiles_all,) + partial_value.shape[2:])
        return lax.psum_scatter(partial_value, "tex", scatter_dimension=0, tiled=True)

    def texel_terms(cotangent):
        gathered = lax.all_gather(cotangent, "tex", axis=0, tiled=True)

        def texel_one_group(members):
            back_part, slot_part, corner_part, frac_part = members
            row_weight, column_weight = tables(
                slot_part, corner_part, frac_part, owner_index, slots
            )
            middle = back_part[:, :, None, :] * column_weight[:, None]
            values = jnp.einsum("tcxp,tjyp->tjcyx", middle, row_weight, precision=exact_mode)
            return values.reshape(values.shape[0] * slots, channels * texels)

        terms = lax.map(texel_one_group, (grouped(gathered),) + pixel_tables)
        return terms.reshape(tiles_all * slots, channels * texels)

    def owner_sums(terms):
        row_count = lax.axis_size("view") * own_blocks
        wanted = jnp.arange(row_count, dtype=jnp.int32)
        selector = (slot_list[None, :] == wanted[:, None]).astype(jnp.float32)
        summed = jnp.dot(selector, terms, precision=exact_mode, preferred_element_type=jnp.float32)
        return lax.psum_scatter(
            summed.reshape(row_count, channels, texels), "view", scatter_dimension=0, tiled=True
        )

    atlas_range = widen(texel_atlas)
    base_params = pixels_of(atlas_range)
    geometry_own = lax.dynamic_slice_in_dim(geometry, owner_index * tiles_own, tiles_own, 0)
    observed_own = lax.dynamic_slice_in_dim(observed, owner_index * tiles_own, tiles_own, 0)

    def render(params):
        return shade(params, geometry_own)

    colors, backward = jax.vjp(render, base_params)

    def pullback(cotangent):
        return backward(cotangent)[0]

    unused, pushed = jax.vjp(pullback, jnp.zeros_like(colors))
    first_terms = texel_terms(backward(colors - observed_own)[0])
    gradient = owner_sums(first_terms)

    def inner_sums(values):
        return lax.psum((values[0],), ("tex", "view"))

    update = jnp.zeros_like(gradient)
    residual = -gradient
    direction = residual
    norm_now = inner_sums((jnp.sum(residual * residual),))[0]
    for iteration in range(ITERS):
        applied = (
            owner_sums(texel_terms(backward(pushed(pixels_of(widen(direction)))[0])[0]))
            + DAMPING * direction
        )
        step_size = norm_now / inner_sums((jnp.sum(direction * applied),))[0]
        update = update + step_size * direction
        residual = residual - step_size * applied
        norm_next = inner_sums((jnp.sum(residual * residual),))[0]
        direction = residual + norm_next / norm_now * direction
        norm_now = norm_next
    return (update, residual)


def solution(mesh):
    in_specs = (
        P(("tex", "view"), None, None),
        P("view", None, None),
        P("view", None, None),
        P("view", "tex", None),
        P("view", None),
        P("view", None),
        P("view", None, None),
    )
    out_specs = (P(("tex", "view"), None, None), P(("tex", "view"), None, None))
    return jax.shard_map(
        per_device, mesh=mesh, in_specs=in_specs, out_specs=out_specs, check_vma=False
    )
```

profile of v0, /device:TPU:0, one launch (start us, length us, event | category | flops | bytes accessed | tf_op | source)
XLA Modules:
  0.0 1119.2 jit_solution(4224892803765773904)
XLA Ops:
  16.4 48.0 %all-gather.4.cloned.1.call-done = f32[16,10,4096]{2,1,0:T(8,128)} async-done(((f32[1,10,4096]{2,1,0:T(8,128)}), f32[16,10,4096]{2,1,0:T(8,128)}) %all-gather.4.cloned.1.call-update) | async-done | bytes 2621456 | tf_op jit(solution)/shard_map/all_gather | solution.py:88
  70.8 9.1 copy_select_fusion.2
  80.0 9.7 reshape.1701
  89.6 23.8 %fusion.13 = f32[8,10,64,768,1]{3,2,1,0,4:T(8,128)} fusion(f32[8,4,10,64,64]{4,3,0,2,1:T(8,128)} %reshape.1701, f32[8,64,768]{2,1,0:T(8,128)S(1)} %select_add_fusion.1, pred[8,4,768]{2,1,0:T(4,128)(4,1)S(1)} %fusion.45), kind=kOutput, calls=%fused_computation.22 | convolution fusion | flops 12081168384 | bytes 22568960 | tf_op jit(solution)/shard_map/while/body/eval_jaxpr/tjcyx,tjyp->tcxp/dot_general | solution.py:99
  113.4 8.8 fusion.8
  127.4 27.1 %reduce-scatter.7.cloned.1.call-done = f32[1,10,768]{2,1,0:T(8,128)} async-done(((f32[8,10,768]{2,1,0:T(8,128)}), f32[1,10,768]{2,1,0:T(8,128)}) %reduce-scatter.7.cloned.1.call-update) | async-done | bytes 30736 | tf_op jit(solution)/shard_map/reduce_scatter | solution.py:104
  161.6 13.0 %all_gather.19 = f32[8,10,768]{2,1,0:T(8,128)S(1)} all-gather(f32[1,10,768]{2,1,0:T(8,128)S(1)} %pad_add_fusion.2), channel_id=1, replica_groups=mesh['tex'=8,'view'=16] {'tex'}, dimensions={0}, use_global_device_ids=true | all-gather | bytes 276480 | tf_op jit(solution)/shard_map/all_gather | solution.py:107
  174.7 29.0 %fusion.27 = f32[8,4,10,64,64]{4,3,2,1,0:T(8,128)} fusion(f32[8,10,768]{2,0,1:T(8,128)S(1)} %copy.51, f32[8,64,768]{2,1,0:T(8,128)S(1)} %select_add_fusion, f32[8,4,64,768,1]{3,2,4,1,0:T(8,128)} %select_bitcast_fusion.20), kind=kOutput, calls=%fused_computation.41 | convolution fusion | flops 12083527680 | bytes 13352960 | tf_op jit(solution)/shard_map/while/body/eval_jaxpr/tcxp,tjyp->tjcyx/dot_general | solution.py:115
  218.3 92.1 %all-reduce.26.cloned.1.call-done = f32[16,10,4096]{2,0,1:T(8,128)} async-done(((f32[16,10,4096]{2,0,1:T(8,128)}), f32[16,10,4096]{2,0,1:T(8,128)}) %all-reduce.26.cloned.1.call-update) | async-done | bytes 2621456
  314.4 50.7 %all-gather.6.cloned.1.call-done = f32[16,10,4096]{2,1,0:T(8,128)} async-done(((f32[1,10,4096]{2,1,0:T(8,128)}), f32[16,10,4096]{2,1,0:T(8,128)}) %all-gather.6.cloned.1.call-update) | async-done | bytes 2621456 | tf_op jit(solution)/shard_map/all_gather | solution.py:88
  371.7 9.1 copy_select_fusion.1
  380.8 9.5 reshape.1703
  390.3 23.7 %fusion.11 = f32[8,10,64,768,1]{3,2,1,0,4:T(8,128)} fusion(f32[8,4,10,64,64]{4,3,0,2,1:T(8,128)} %reshape.1703, f32[8,64,768]{2,1,0:T(8,128)S(1)} %select_add_fusion.1, pred[8,4,768]{2,1,0:T(4,128)(4,1)S(1)} %fusion.45), kind=kOutput, calls=%fused_computation.20 | convolution fusion | flops 12081168384 | bytes 22568960 | tf_op jit(solution)/shard_map/while/body/eval_jaxpr/tjcyx,tjyp->tcxp/dot_general | solution.py:99
  414.0 8.8 fusion.5
  428.0 27.1 %reduce-scatter.9.cloned.1.call-done = f32[1,10,768]{2,1,0:T(8,128)} async-done(((f32[8,10,768]{2,1,0:T(8,128)}), f32[1,10,768]{2,1,0:T(8,128)}) %reduce-scatter.9.cloned.1.call-update) | async-done | bytes 30736 | tf_op jit(solution)/shard_map/reduce_scatter | solution.py:104
  459.1 13.0 %all_gather.21 = f32[8,10,768]{2,1,0:T(8,128)S(1)} all-gather(f32[1,10,768]{2,1,0:T(8,128)S(1)} %pad_add_fusion.1), channel_id=1, replica_groups=mesh['tex'=8,'view'=16] {'tex'}, dimensions={0}, use_global_device_ids=true | all-gather | bytes 276480 | tf_op jit(solution)/shard_map/all_gather | solution.py:107
  472.2 29.0 %fusion.30 = f32[8,4,10,64,64]{4,3,2,1,0:T(8,128)} fusion(f32[8,10,768]{2,0,1:T(8,128)S(1)} %copy.60, f32[8,64,768]{2,1,0:T(8,128)S(1)} %select_add_fusion, f32[8,4,64,768,1]{3,2,4,1,0:T(8,128)} %select_bitcast_fusion.21), kind=kOutput, calls=%fused_computation.42 | convolution fusion | flops 12083527680 | bytes 13352960 | tf_op jit(solution)/shard_map/while/body/eval_jaxpr/tcxp,tjyp->tjcyx/dot_general | solution.py:115
  501.2 7.9 reshape.1704
  515.2 92.8 %all-reduce.28.cloned.1.call-done = f32[16,10,4096]{2,0,1:T(8,128)} async-done(((f32[16,10,4096]{2,0,1:T(8,128)}), f32[16,10,4096]{2,0,1:T(8,128)}) %all-reduce.28.cloned.1.call-update) | async-done | bytes 2621456
  611.0 64.5 %all-reduce.21 = (f32[]{:T(128)}, f32[]{:T(128)}) all-reduce(f32[]{:T(128)} %get-tuple-element.217, f32[]{:T(128)} %multiply_reduce_fusion.2), channel_id=1, replica_groups=mesh['tex'=8,'view'=16] {'tex','view'}, use_global_device_ids=true, to_apply=%region_8.10 | all-reduce | flops 2 | bytes 16 | tf_op jit(solution)/shard_map/psum | solution.py:148
  680.4 62.7 %psum.30 = f32[]{:T(128)} all-reduce(f32[]{:T(128)} %get-tuple-element.169), channel_id=1, replica_groups=mesh['tex'=8,'view'=16] {'tex','view'}, use_global_device_ids=true, to_apply=%region_17.19 | all-reduce | flops 1 | bytes 8 | tf_op jit(solution)/shard_map/psum | solution.py:148
  746.6 48.7 %all-gather.8.cloned.1.call-done = f32[16,10,4096]{2,1,0:T(8,128)} async-done(((f32[1,10,4096]{2,1,0:T(8,128)}), f32[16,10,4096]{2,1,0:T(8,128)}) %all-gather.8.cloned.1.call-update) | async-done | bytes 2621456 | tf_op jit(solution)/shard_map/all_gather | solution.py:88
  801.7 9.1 copy_select_fusion
  810.9 9.5 reshape.1705
  820.4 23.5 %fusion.9 = f32[8,10,64,768,1]{3,2,1,0,4:T(8,128)} fusion(f32[8,4,10,64,64]{4,3,0,2,1:T(8,128)} %reshape.1705, f32[8,64,768]{2,1,0:T(8,128)S(1)} %select_add_fusion.1, pred[8,4,768]{2,1,0:T(4,128)(4,1)S(1)} %copy-done.3), kind=kOutput, calls=%fused_computation.18 | convolution fusion | flops 12081168384 | bytes 22568960 | tf_op jit(solution)/shard_map/while/body/eval_jaxpr/tjcyx,tjyp->tcxp/dot_general | solution.py:99
  843.9 8.8 fusion.2
  857.9 27.1 %reduce-scatter.11.cloned.1.call-done = f32[1,10,768]{2,1,0:T(8,128)} async-done(((f32[8,10,768]{2,1,0:T(8,128)}), f32[1,10,768]{2,1,0:T(8,128)}) %reduce-scatter.11.cloned.1.call-update) | async-done | bytes 30736 | tf_op jit(solution)/shard_map/reduce_scatter | solution.py:104
  891.5 13.0 %all_gather.23 = f32[8,10,768]{2,1,0:T(8,128)S(1)} all-gather(f32[1,10,768]{2,1,0:T(8,128)S(1)} %pad_add_fusion), channel_id=1, replica_groups=mesh['tex'=8,'view'=16] {'tex'}, dimensions={0}, use_global_device_ids=true | all-gather | bytes 276480 | tf_op jit(solution)/shard_map/all_gather | solution.py:107
  904.6 29.0 %fusion.33 = f32[8,4,10,64,64]{4,3,2,1,0:T(8,128)} fusion(f32[8,10,768]{2,0,1:T(8,128)S(1)} %copy.69, f32[8,64,768]{2,1,0:T(8,128)S(1)} %select_add_fusion, f32[8,4,64,768,1]{3,2,4,1,0:T(8,128)} %select_bitcast_fusion.22), kind=kOutput, calls=%fused_computation.43 | convolution fusion | flops 12083527680 | bytes 13352960 | tf_op jit(solution)/shard_map/while/body/eval_jaxpr/tcxp,tjyp->tjcyx/dot_general | solution.py:115
  933.6 7.9 reshape.1706
  947.6 92.9 %all-reduce.30.cloned.1.call-done = f32[16,10,4096]{2,0,1:T(8,128)} async-done(((f32[16,10,4096]{2,0,1:T(8,128)}), f32[16,10,4096]{2,0,1:T(8,128)}) %all-reduce.30.cloned.1.call-update) | async-done | bytes 2621456
  1043.4 64.4 %psum.31 = f32[]{:T(128)} all-reduce(f32[]{:T(128)} %multiply_reduce_fusion), channel_id=1, replica_groups=mesh['tex'=8,'view'=16] {'tex','view'}, use_global_device_ids=true, to_apply=%region_24.26 | all-reduce | flops 1 | bytes 8 | tf_op jit(solution)/shard_map/psum | solution.py:148
  (196 shorter events, 106.6 us)
Async XLA Ops:
  7.2 57.1 %all-gather.4.cloned.1.call-start = ((), (), s32[]{:S(2)}) async-start(), calls=%async_computation.3 | async-start | bytes 4456448 | tf_op jit(solution)/shard_map/all_gather | solution.py:88
  9.0 145.5 %reduce-scatter.7.cloned.1.call-start = ((), (), s32[]{:S(2)}) async-start(), calls=%async_computation.4 | async-start | bytes 442368 | tf_op jit(solution)/shard_map/reduce_scatter | solution.py:104
  11.7 353.5 %copy-start.16 = (s32[1024]{0:T(1024)}, s32[1024]{0:T(1024)S(1)}, u32[]{:S(2)}) copy-start(s32[1024]{0:T(1024)S(1)} %pad_clamp_fusion) | copy-start | bytes 12292
  11.7 446.3 %copy-start.6 = (f32[1,3,768]{2,1,0:T(4,128)}, f32[1,3,768]{2,1,0:T(4,128)S(1)}, u32[]{:S(2)}) copy-start(f32[1,3,768]{2,1,0:T(4,128)S(1)} %get-tuple-element.214) | copy-start | bytes 27652
  14.1 410.6 %copy-start.2 = (pred[8,4,768]{2,1,0:T(4,128)(4,1)}, pred[8,4,768]{2,1,0:T(4,128)(4,1)S(1)}, u32[]{:S(2)}) copy-start(pred[8,4,768]{2,1,0:T(4,128)(4,1)S(1)} %fusion.45) | copy-start | bytes 73732
  124.0 186.4 %all-reduce.26.cloned.1.call-start = ((), (), s32[]{:S(2)}) async-start(), calls=%async_computation.9 | async-start | bytes 5242880
  155.5 300.5 %copy-start.26 = (f32[768]{0:T(1024)}, f32[768]{0:T(1024)S(1)}, u32[]{:S(2)}) copy-start(f32[768]{0:T(1024)S(1)} %get-tuple-element.87) | copy-start | bytes 9220
  155.5 300.5 %copy-start.27 = (f32[768]{0:T(1024)}, f32[768]{0:T(1024)S(1)}, u32[]{:S(2)}) copy-start(f32[768]{0:T(1024)S(1)} %get-tuple-element.88) | copy-start | bytes 9220
  155.5 300.5 %copy-start.28 = (f32[768]{0:T(1024)}, f32[768]{0:T(1024)S(1)}, u32[]{:S(2)}) copy-start(f32[768]{0:T(1024)S(1)} %get-tuple-element.89) | copy-start | bytes 9220
  155.5 300.5 %copy-start.29 = (f32[768]{0:T(1024)}, f32[768]{0:T(1024)S(1)}, u32[]{:S(2)}) copy-start(f32[768]{0:T(1024)S(1)} %get-tuple-element.90) | copy-start | bytes 9220
  155.5 300.5 %copy-start.30 = (f32[768]{0:T(1024)}, f32[768]{0:T(1024)S(1)}, u32[]{:S(2)}) copy-start(f32[768]{0:T(1024)S(1)} %get-tuple-element.98) | copy-start | bytes 9220
  155.5 300.5 %copy-start.31 = (f32[768]{0:T(1024)}, f32[768]{0:T(1024)S(1)}, u32[]{:S(2)}) copy-start(f32[768]{0:T(1024)S(1)} %get-tuple-element.99) | copy-start | bytes 9220
  155.6 300.5 %copy-start.32 = (f32[768]{0:T(1024)}, f32[768]{0:T(1024)S(1)}, u32[]{:S(2)}) copy-start(f32[768]{0:T(1024)S(1)} %get-tuple-element.221) | copy-start | bytes 9220
  155.6 300.5 %copy-start.33 = (f32[768]{0:T(1024)}, f32[768]{0:T(1024)S(1)}, u32[]{:S(2)}) copy-start(f32[768]{0:T(1024)S(1)} %get-tuple-element.222) | copy-start | bytes 9220
  155.6 300.5 %copy-start.34 = (f32[768]{0:T(1024)}, f32[768]{0:T(1024)S(1)}, u32[]{:S(2)}) copy-start(f32[768]{0:T(1024)S(1)} %get-tuple-element.223) | copy-start | bytes 9220
  155.6 300.5 %copy-start.35 = (f32[768]{0:T(1024)}, f32[768]{0:T(1024)S(1)}, u32[]{:S(2)}) copy-start(f32[768]{0:T(1024)S(1)} %get-tuple-element.224) | copy-start | bytes 9220
  155.6 301.5 %copy-start.7 = (f32[768]{0:T(1024)}, f32[768]{0:T(1024)S(1)}, u32[]{:S(2)}) copy-start(f32[768]{0:T(1024)S(1)} %get-tuple-element.225) | copy-start | bytes 9220
  155.6 303.3 %copy-start.8 = (f32[1,1,768]{2,1,0:T(1,128)}, f32[1,1,768]{2,1,0:T(1,128)S(1)}, u32[]{:S(2)}) copy-start(f32[1,1,768]{2,1,0:T(1,128)S(1)} %get-tuple-element.227) | copy-start | bytes 9220
  155.6 303.3 %copy-start.9 = (f32[1,1,768]{2,1,0:T(1,128)}, f32[1,1,768]{2,1,0:T(1,128)S(1)}, u32[]{:S(2)}) copy-start(f32[1,1,768]{2,1,0:T(1,128)S(1)} %get-tuple-element.226) | copy-start | bytes 9220
  155.7 300.5 %copy-start.25 = (f32[768]{0:T(1024)}, f32[768]{0:T(1024)S(1)}, u32[]{:S(2)}) copy-start(f32[768]{0:T(1024)S(1)} %get-tuple-element.212) | copy-start | bytes 9220
  155.7 301.4 %copy-start.18 = (f32[768]{0:T(1024)}, f32[768]{0:T(1024)S(1)}, u32[]{:S(2)}) copy-start(f32[768]{0:T(1024)S(1)} %get-tuple-element.211) | copy-start | bytes 9220
  158.3 300.6 %copy-start.11 = (f32[1,1,768]{2,1,0:T(1,128)}, f32[1,1,768]{2,1,0:T(1,128)S(1)}, u32[]{:S(2)}) copy-start(f32[1,1,768]{2,1,0:T(1,128)S(1)} %get-tuple-element.200) | copy-start | bytes 9220
  158.3 300.6 %copy-start.12 = (f32[1,1,768]{2,1,0:T(1,128)}, f32[1,1,768]{2,1,0:T(1,128)S(1)}, u32[]{:S(2)}) copy-start(f32[1,1,768]{2,1,0:T(1,128)S(1)} %get-tuple-element.201) | copy-start | bytes 9220
  158.3 300.6 %copy-start.13 = (f32[1,1,768]{2,1,0:T(1,128)}, f32[1,1,768]{2,1,0:T(1,128)S(1)}, u32[]{:S(2)}) copy-start(f32[1,1,768]{2,1,0:T(1,128)S(1)} %get-tuple-element.202) | copy-start | bytes 9220
  158.3 300.6 %copy-start.14 = (f32[1,1,768]{2,1,0:T(1,128)}, f32[1,1,768]{2,1,0:T(1,128)S(1)}, u32[]{:S(2)}) copy-start(f32[1,1,768]{2,1,0:T(1,128)S(1)} %get-tuple-element.206) | copy-start | bytes 9220
  158.3 300.6 %copy-start.15 = (f32[1,1,768]{2,1,0:T(1,128)}, f32[1,1,768]{2,1,0:T(1,128)S(1)}, u32[]{:S(2)}) copy-start(f32[1,1,768]{2,1,0:T(1,128)S(1)} %get-tuple-element.207) | copy-start | bytes 9220
  217.6 147.5 %all-gather.6.cloned.1.call-start = ((), (), s32[]{:S(2)}) async-start(), calls=%async_computation.5 | async-start | bytes 4456448 | tf_op jit(solution)/shard_map/all_gather | solution.py:88
  314.2 140.9 %reduce-scatter.9.cloned.1.call-start = ((), (), s32[]{:S(2)}) async-start(), calls=%async_computation.6 | async-start | bytes 442368 | tf_op jit(solution)/shard_map/reduce_scatter | solution.py:104
  424.7 183.3 %all-reduce.28.cloned.1.call-start = ((), (), s32[]{:S(2)}) async-start(), calls=%async_computation.10 | async-start | bytes 5242880
  515.1 280.1 %all-gather.8.cloned.1.call-start = ((), (), s32[]{:S(2)}) async-start(), calls=%async_computation.7 | async-start | bytes 4456448 | tf_op jit(solution)/shard_map/all_gather | solution.py:88
  746.5 138.5 %reduce-scatter.11.cloned.1.call-start = ((), (), s32[]{:S(2)}) async-start(), calls=%async_computation.8 | async-start | bytes 442368 | tf_op jit(solution)/shard_map/reduce_scatter | solution.py:104
  854.5 185.9 %all-reduce.30.cloned.1.call-start = ((), (), s32[]{:S(2)}) async-start(), calls=%async_computation.11 | async-start | bytes 5242880
  (28 other events, 3623.3 us)
Sparse Core Ops, SparseCore 0:
  10.2 54.1 all-gather.3
  124.2 30.2 reduce-scatter.6
  217.7 92.6 all-reduce.25
  314.3 50.8 all-gather.5
  424.8 30.2 reduce-scatter.8
  515.2 92.6 all-reduce.27
  746.6 48.5 all-gather.7
  854.7 30.2 reduce-scatter.10
  947.7 92.6 all-reduce.29
where the time goes:
time: 1130 us; the launch traced here: 1120 us
  waiting for transfers between devices  507 us (45%)
  blocking collectives  230 us (20%)
  matrix products  176 us (16%)
  other arithmetic  102 us (9%)
  local copies, waits for them, and re-layouts  84.7 us (7%)
  between operations  19.1 us (2%)
    unnamed x12, waiting for transfers between devices  278 us
    psum x3, blocking collectives, inner_sums(): return lax.psum((values[0],), ('tex', 'view'))  191 us
    all_gather x3, waiting for transfers between devices, widen(): return lax.all_gather(own_shard, 'view', axis=0, tiled=True)  147 us
    dot_general x3, matrix products, texel_one_group(): jnp.einsum('tcxp,tjyp->tjcyx', middle, row_weight, precision=exact_mode)  87.1 us
    reduce_scatter x3, waiting for transfers between devices, pixels_of(): lax.psum_scatter(partial_value, 'tex', scatter_dimension=0, tiled=True)  81.4 us
    dot_general x3, matrix products, pixels_one_group(): jnp.einsum('tjcyx,tjyp->tcxp', values, row_weight, precision=exact_mode)  71.1 us
    all_gather x3, blocking collectives, texel_terms(): gathered = lax.all_gather(cotangent, 'tex', axis=0, tiled=True)  38.9 us
    reshape x3, local copies, waits for them, and re-layouts, pixels_one_group(): values = blocks.reshape(blocks.shape[0], slots, channels, BSIDE, BSIDE)  28.7 us
  transfers between devices with their start and end apart: 9, of which 9 were waited for; matrix products, arithmetic and copies ran while one was open for 2% of the time, Pallas kernels for 0%

commit v1 on v0

--- a/solution.py
+++ b/solution.py
@@ -1,8 +1,11 @@
+import functools
 import math
 
 import jax
 import jax.numpy as jnp
 from jax import lax
+from jax.experimental import pallas as pl
+from jax.experimental.pallas import tpu as pltpu
 from jax.sharding import PartitionSpec as P
 
 BSIDE = 64
@@ -67,7 +70,7 @@
     return (row_weight, column_weight)
 
 
-def per_device(texel_atlas, observed, geometry, block_ids, pixel_slot, corner, bilinear_frac):
+def general_step(texel_atlas, observed, geometry, block_ids, pixel_slot, corner, bilinear_frac):
     tex_count = lax.axis_size("tex")
     owner_index = lax.axis_index("tex")
     own_blocks, channels, texels = texel_atlas.shape
@@ -88,7 +91,11 @@
         return lax.all_gather(own_shard, "view", axis=0, tiled=True)
 
     def pixels_of(whole_range):
-        fetched = jnp.take(whole_range, jnp.clip(slot_blocks, 0, whole_range.shape[0] - 1), axis=0)
+        ranged = whole_range.shape[0]
+        named = jnp.arange(ranged, dtype=jnp.int32)
+        chooser = (jnp.clip(slot_list, 0, ranged - 1)[:, None] == named[None, :]).astype(jnp.float32)
+        fetched = jnp.dot(chooser, whole_range.reshape(ranged, -1), precision=exact_mode)
+        fetched = fetched.reshape(tiles_all, slots, channels, texels)
 
         def pixels_one_group(members):
             blocks, slot_part, corner_part, frac_part = members
@@ -163,6 +170,514 @@
         direction = residual + norm_next / norm_now * direction
         norm_now = norm_next
     return (update, residual)
+
+
+MESH = pl.DeviceIdType.MESH
+F32 = jnp.float32
+BF16 = jnp.bfloat16
+CHANNELS = 10
+ROWS = 16
+WINDOW = 384
+PICKED = 256
+SORTED = 1024
+CHUNK = 256
+NT = (((1,), (1,)), ((), ()))
+
+
+def halves(values):
+    high = values.astype(BF16)
+    low = (values - high.astype(F32)).astype(BF16)
+    return high, low
+
+
+def iota(shape, axis):
+    return lax.broadcasted_iota(jnp.int32, shape, axis)
+
+
+def pack_kernel(ids, obs, geo, frac, slot, corner, out, spilled, picked, ordered):
+    tiles, pixels = slot.shape
+    slots = ids.shape[0]
+    blocks = out.shape[0]
+    owner = lax.axis_index("tex")
+    lanes = pixels // 128
+
+    slot_now = slot[...]
+    corner_now = corner[...]
+    row = corner_now // (BSIDE - 1)
+    column = (corner_now - row * (BSIDE - 1)).astype(F32)
+    row = row.astype(F32)
+    tile_of = iota((tiles, 128), 0)
+    target = jnp.zeros((tiles, pixels), jnp.int32)
+    for s in range(slots):
+        named = jnp.zeros((tiles, 128), jnp.int32)
+        for t in range(tiles):
+            named = jnp.where(tile_of == t, ids[s, t] + 1, named)
+        target = jnp.where(
+            slot_now == owner * slots + s, jnp.concatenate([named] * lanes, axis=1), target
+        )
+    mine = jnp.where(target > 0, 1.0, 0.0)
+    before = jnp.where(iota((128, 128), 0) < iota((128, 128), 1), 1.0, 0.0).astype(BF16)
+
+    stacked = jnp.concatenate([mine[:, c * 128 : c * 128 + 128] for c in range(lanes)], axis=0)
+    ahead = jnp.dot(stacked.astype(BF16), before, preferred_element_type=F32)
+    base = jnp.zeros((tiles, 1), F32)
+    places = []
+    for c in range(lanes):
+        places.append(ahead[c * tiles : c * tiles + tiles] + base)
+        base = base + jnp.sum(mine[:, c * 128 : c * 128 + 128], axis=1, keepdims=True)
+    place = jnp.where(target > 0, jnp.concatenate(places, axis=1), -1.0).astype(jnp.int32)
+    over = jnp.max(jnp.where(base > PICKED, 1.0, 0.0))
+    total = jnp.sum(base)
+    over = jnp.maximum(over, jnp.where(total > SORTED, 1.0, 0.0))
+
+    target_f = target.astype(F32)
+    wanted = iota((PICKED, pixels), 0)
+    for t in range(tiles):
+        numbers = jnp.concatenate(
+            [
+                obs[:, t, :],
+                geo[:, t, :],
+                frac[t],
+                row[t : t + 1],
+                column[t : t + 1],
+                target_f[t : t + 1],
+                jnp.zeros((2, pixels), F32),
+            ],
+            axis=0,
+        )
+        both = jnp.concatenate(halves(numbers), axis=0)
+        hot = jnp.where(wanted == place[t : t + 1], 1.0, 0.0).astype(BF16)
+        got = lax.dot_general(both, hot, NT, preferred_element_type=F32)
+        picked[:, t * PICKED : t * PICKED + PICKED] = got[:ROWS] + got[ROWS:]
+
+    listed = tiles * PICKED
+    groups = listed // 128
+    target_row = picked[13:14, :]
+    member = jnp.where(
+        iota((blocks, listed), 0).astype(F32) + 1.0 == target_row, 1.0, 0.0
+    )
+    stacked = jnp.concatenate([member[:, c * 128 : c * 128 + 128] for c in range(groups)], axis=0)
+    ahead = jnp.dot(stacked.astype(BF16), before, preferred_element_type=F32)
+    base = jnp.zeros((blocks, 1), F32)
+    places = []
+    for c in range(groups):
+        places.append(ahead[c * blocks : c * blocks + blocks] + base)
+        base = base + jnp.sum(member[:, c * 128 : c * 128 + 128], axis=1, keepdims=True)
+    over = jnp.maximum(over, jnp.max(jnp.where(base > WINDOW, 1.0, 0.0)))
+    earlier = jnp.where(iota((blocks, blocks), 1) < iota((blocks, blocks), 0), 1.0, 0.0)
+    first = jnp.dot(
+        earlier,
+        jnp.broadcast_to(base, (blocks, 128)),
+        precision=lax.Precision.HIGHEST,
+        preferred_element_type=F32,
+    )
+    place = jnp.concatenate(places, axis=1) + first[:, 0:1]
+    place = jnp.sum(member * place, axis=0, keepdims=True)
+    place = jnp.where(target_row > 0.0, place, -1.0).astype(jnp.int32)
+    both = jnp.concatenate(halves(picked[...]), axis=0)
+    ordered[:, SORTED:] = jnp.zeros((ROWS, ordered.shape[1] - SORTED), F32)
+    for q in range(SORTED // 256):
+        hot = jnp.where(iota((256, listed), 0) + q * 256 == place, 1.0, 0.0).astype(BF16)
+        got = lax.dot_general(both, hot, NT, preferred_element_type=F32)
+        ordered[:, q * 256 : q * 256 + 256] = got[:ROWS] + got[ROWS:]
+
+    first = jnp.minimum(first, float(SORTED)).astype(jnp.int32)
+    wide = WINDOW + 128
+    for k in range(blocks):
+        begin = first[k, 0]
+        aligned = pl.multiple_of(begin // 128 * 128, 128)
+        window = ordered[:, pl.ds(aligned, wide)]
+        shift = begin - aligned
+        window = pltpu.roll(window, lax.rem(wide - shift, wide), axis=1)
+        out[k] = window[:, :WINDOW]
+    spilled[...] = jnp.full(spilled.shape, over, F32)
+
+
+def exchange_kernel(windows, landed, own_sem, send_sem, recv_sem):
+    tex = lax.axis_index("tex")
+    view = lax.axis_index("view")
+    views = windows.shape[0]
+    barrier = pltpu.get_barrier_semaphore()
+    for step in range(1, views):
+        peer = lax.rem(view + step, views)
+        pl.semaphore_signal(barrier, inc=1, device_id=(tex, peer), device_id_type=MESH)
+    own = pltpu.make_async_copy(windows.at[view], landed.at[view], own_sem)
+    own.start()
+    pl.semaphore_wait(barrier, views - 1)
+    copies = []
+    for step in range(1, views):
+        peer = lax.rem(view + step, views)
+        copy = pltpu.make_async_remote_copy(
+            src_ref=windows.at[peer],
+            dst_ref=landed.at[view],
+            send_sem=send_sem.at[step],
+            recv_sem=recv_sem.at[step],
+            device_id=(tex, peer),
+            device_id_type=MESH,
+        )
+        copy.start()
+        copies.append(copy)
+    own.wait()
+    for copy in copies:
+        copy.wait()
+
+
+def optics(params, geometry):
+    roughness, tilt_x, tilt_y, occlusion = params[6], params[7], params[8], params[9]
+    light, viewer = geometry[0:3], geometry[3:6]
+    inverse_len = lax.rsqrt(1.0 + tilt_x * tilt_x + tilt_y * tilt_y)
+    normal_x = tilt_x * inverse_len
+    normal_y = tilt_y * inverse_len
+    half = [a + b for a, b in zip(light, viewer)]
+    scale = lax.rsqrt(half[0] * half[0] + half[1] * half[1] + half[2] * half[2])
+    half = [a * scale for a in half]
+
+    def facing(vector):
+        cosine = normal_x * vector[0] + normal_y * vector[1] + inverse_len * vector[2]
+        along_x = inverse_len * (vector[0] - normal_x * cosine)
+        along_y = inverse_len * (vector[1] - normal_y * cosine)
+        return cosine, along_x, along_y
+
+    light_c, light_x, light_y = facing(light)
+    view_c, view_x, view_y = facing(viewer)
+    half_c, half_x, half_y = facing(half)
+    miss = 1.0 - (viewer[0] * half[0] + viewer[1] * half[1] + viewer[2] * half[2])
+    fifth = miss * miss
+    fifth = fifth * fifth * miss
+    square = roughness * roughness
+    fourth = square * square
+    inverse_d = 1.0 / (half_c * half_c * (fourth - 1.0) + 1.0)
+    smith = 0.5 * square
+    inverse_l = 1.0 / (light_c * (1.0 - smith) + smith)
+    inverse_v = 1.0 / (view_c * (1.0 - smith) + smith)
+    shape = 0.25 * inverse_d * inverse_d * inverse_l * inverse_v
+    gloss = fourth * shape
+    shape_slope = -4.0 * square * half_c * half_c * inverse_d
+    shape_slope = shape_slope - 0.5 * (1.0 - light_c) * inverse_l - 0.5 * (1.0 - view_c) * inverse_v
+    gloss_square = 2.0 * square * shape + gloss * shape_slope
+    gloss_half = -4.0 * gloss * half_c * (fourth - 1.0) * inverse_d
+    gloss_light = -gloss * (1.0 - smith) * inverse_l
+    gloss_view = -gloss * (1.0 - smith) * inverse_v
+    gloss_x = gloss_half * half_x + gloss_light * light_x + gloss_view * view_x
+    gloss_y = gloss_half * half_y + gloss_light * light_y + gloss_view * view_y
+    lit = occlusion * light_c
+    fresnel = [params[3 + c] + (1.0 - params[3 + c]) * fifth for c in range(3)]
+    total = [params[c] + gloss * fresnel[c] for c in range(3)]
+    factors = [
+        lit,
+        lit * gloss * (1.0 - fifth),
+        lit * gloss_square * 2.0 * roughness,
+        occlusion * light_x,
+        lit * gloss_x,
+        occlusion * light_y,
+        lit * gloss_y,
+        light_c,
+    ]
+    return factors + total + fresnel, [lit * t for t in total]
+
+
+def push(tangent, factors):
+    albedo, specular, rough, ex, fx, ey, fy, shine = factors[:8]
+    total, fresnel = factors[8:11], factors[11:14]
+    on_total = ex * tangent[7] + ey * tangent[8] + shine * tangent[9]
+    on_fresnel = rough * tangent[6] + fx * tangent[7] + fy * tangent[8]
+    return [
+        albedo * tangent[c] + specular * tangent[3 + c] + total[c] * on_total + fresnel[c] * on_fresnel
+        for c in range(3)
+    ]
+
+
+def pull(colors, factors):
+    albedo, specular, rough, ex, fx, ey, fy, shine = factors[:8]
+    total, fresnel = factors[8:11], factors[11:14]
+    e = total[0] * colors[0] + total[1] * colors[1] + total[2] * colors[2]
+    f = fresnel[0] * colors[0] + fresnel[1] * colors[1] + fresnel[2] * colors[2]
+    return (
+        [albedo * c for c in colors]
+        + [specular * c for c in colors]
+        + [rough * f, ex * e + fx * f, ey * e + fy * f, shine * e]
+    )
+
+
+def solve_kernel(
+    landed, spilled, atlas, start, first, second, sums, pixels, field, across, down, slopes, gathered
+):
+    senders = landed.shape[0]
+    me = lax.axis_index("view")
+    half_rows = CHANNELS * BSIDE // 2
+    lane = iota((half_rows, 128), 1)
+
+    pixels[...] = jnp.zeros(pixels.shape, F32)
+    marks = landed[:, 13, :]
+    live = jnp.where(marks == (me + 1).astype(F32), 1.0, 0.0)
+    counts = jnp.sum(live, axis=1, keepdims=True)
+    earlier = jnp.where(iota((senders, senders), 1) < iota((senders, senders), 0), 1.0, 0.0)
+    begins = jnp.dot(
+        earlier,
+        jnp.broadcast_to(counts, (senders, 128)),
+        precision=lax.Precision.HIGHEST,
+        preferred_element_type=F32,
+    ).astype(jnp.int32)
+    wide = WINDOW + 128
+    for j in range(senders):
+        begin = begins[j, 0]
+        aligned = pl.multiple_of(begin // 128 * 128, 128)
+        window = jnp.where(live[j : j + 1] > 0.0, landed[j], 0.0)
+        window = jnp.concatenate([window, jnp.zeros((ROWS, 128), F32)], axis=1)
+        window = pltpu.roll(window, begin - aligned, axis=1)
+        pixels[:, pl.ds(aligned, wide)] += window
+    count = jnp.sum(counts).astype(jnp.int32)
+    chunks = (count + CHUNK - 1) // CHUNK
+
+    def hold(values):
+        high, low = halves(values)
+        high, low = high.astype(F32), low.astype(F32)
+        left = jnp.where(lane < BSIDE, high, pltpu.roll(low, BSIDE, axis=1)).astype(BF16)
+        right = jnp.where(lane < BSIDE, pltpu.roll(high, BSIDE, axis=1), low).astype(BF16)
+        field[:half_rows, :128] = left
+        field[:half_rows, 128:] = left
+        field[half_rows:, :128] = right
+        field[half_rows:, 128:] = right
+
+    def sample(c, rows):
+        seen = jnp.dot(field[...], across[c], preferred_element_type=F32)
+        seen = seen.reshape(2, CHANNELS, BSIDE // 2, CHUNK) * rows
+        seen = jnp.sum(seen[0] + seen[1], axis=1)
+        return [seen[k : k + 1] for k in range(CHANNELS)]
+
+    def spread(c, rows, back):
+        back = jnp.concatenate(back, axis=0)
+        terms = (back.reshape(1, CHANNELS, 1, CHUNK) * rows).reshape(2 * half_rows, CHUNK)
+        high, low = halves(terms)
+        columns = across[c, BSIDE : 3 * BSIDE, :]
+        gathered[...] += lax.dot_general(high, columns, NT, preferred_element_type=F32)
+        gathered[...] += lax.dot_general(low, columns, NT, preferred_element_type=F32)
+
+    def collected():
+        left, right = gathered[:half_rows], gathered[half_rows:]
+        left = left + pltpu.roll(left, BSIDE, axis=1)
+        right = right + pltpu.roll(right, BSIDE, axis=1)
+        return jnp.where(lane < BSIDE, left, right)
+
+    hold(atlas[...])
+    gathered[...] = jnp.zeros(gathered.shape, F32)
+
+    def first_pass(c, carry):
+        numbers = pixels[:, pl.ds(pl.multiple_of(c * CHUNK, CHUNK), CHUNK)]
+        numbers = [numbers[k : k + 1] for k in range(ROWS)]
+        used = iota((1, CHUNK), 1) + c * CHUNK < count
+        frac_x, frac_y, row, column = numbers[9:13]
+        at = iota((BSIDE, CHUNK), 0).astype(F32)
+        weight = jnp.where(at == column, 1.0 - frac_x, jnp.where(at == column + 1.0, frac_x, 0.0))
+        high, low = halves(weight)
+        across[c] = jnp.concatenate([high, high, low, low], axis=0)
+        at = iota((BSIDE, CHUNK), 0)
+        at = jnp.where(at < BSIDE // 2, 2 * at, 2 * at - (BSIDE - 1)).astype(F32)
+        weight = jnp.where(at == row, 1.0 - frac_y, jnp.where(at == row + 1.0, frac_y, 0.0))
+        weight = jnp.where(used, weight, 0.0)
+        down[c] = weight
+        rows = weight.reshape(2, 1, BSIDE // 2, CHUNK)
+        factors, colors = optics(sample(c, rows), numbers[3:9])
+        factors = [jnp.where(used, factor, 0.0) for factor in factors]
+        slopes[c] = jnp.concatenate(factors + [jnp.zeros((2, CHUNK), F32)], axis=0)
+        errors = [jnp.where(used, a - b, 0.0) for a, b in zip(colors, numbers[0:3])]
+        spread(c, rows, pull(errors, factors))
+        return carry
+
+    lax.fori_loop(0, chunks, first_pass, 0)
+    start_now = -collected()
+    start[...] = start_now
+
+    def applied(values):
+        hold(values)
+        gathered[...] = jnp.zeros(gathered.shape, F32)
+
+        def one_pass(c, carry):
+            rows = down[c].reshape(2, 1, BSIDE // 2, CHUNK)
+            factors = slopes[c]
+            factors = [factors[k : k + 1] for k in range(14)]
+            spread(c, rows, pull(push(sample(c, rows), factors), factors))
+            return carry
+
+        lax.fori_loop(0, chunks, one_pass, 0)
+        return collected() + DAMPING * values
+
+    first_now = applied(start_now)
+    first[...] = first_now
+    second_now = applied(first_now)
+    second[...] = second_now
+
+    start_start = jnp.sum(start_now * start_now)
+    start_first = jnp.sum(start_now * first_now)
+    guess = jnp.where(start_first > 0.0, start_start / jnp.where(start_first > 0.0, start_first, 1.0), 0.0)
+    rest = start_now - guess * first_now
+    image = first_now - guess * second_now
+    found = [
+        start_start,
+        start_first,
+        jnp.sum(rest * rest),
+        jnp.sum(rest * first_now),
+        jnp.sum(first_now * first_now),
+        jnp.sum(rest * image),
+        jnp.sum(image * first_now),
+        jnp.sum(first_now * second_now),
+        guess,
+    ]
+    place = iota((1, 128), 1)
+    line = jnp.where(place == len(found), spilled[...], 0.0)
+    for k, value in enumerate(found):
+        line = jnp.where(place == k, value, line)
+    sums[...] = line
+
+
+def steps_kernel(sums, steps, near, far, send_near, recv_near, send_far, recv_far):
+    tex = lax.axis_index("tex")
+    view = lax.axis_index("view")
+    owners, views = near.shape[0], far.shape[0]
+    barrier = pltpu.get_barrier_semaphore()
+    for step in range(1, owners):
+        peer = lax.rem(tex + step, owners)
+        pl.semaphore_signal(barrier, inc=1, device_id=(peer, view), device_id_type=MESH)
+    for step in range(1, views):
+        peer = lax.rem(view + step, views)
+        pl.semaphore_signal(barrier, inc=1, device_id=(tex, peer), device_id_type=MESH)
+    near[tex] = sums[...]
+    pl.semaphore_wait(barrier, owners + views - 2)
+    copies = []
+    for step in range(1, owners):
+        peer = lax.rem(tex + step, owners)
+        copy = pltpu.make_async_remote_copy(
+            src_ref=sums,
+            dst_ref=near.at[tex],
+            send_sem=send_near.at[step],
+            recv_sem=recv_near.at[step],
+            device_id=(peer, view),
+            device_id_type=MESH,
+        )
+        copy.start()
+        copies.append(copy)
+    for copy in copies:
+        copy.wait()
+    far[view] = near[...]
+    copies = []
+    for step in range(1, views):
+        peer = lax.rem(view + step, views)
+        copy = pltpu.make_async_remote_copy(
+            src_ref=near,
+            dst_ref=far.at[view],
+            send_sem=send_far.at[step],
+            recv_sem=recv_far.at[step],
+            device_id=(tex, peer),
+            device_id_type=MESH,
+        )
+        copy.start()
+        copies.append(copy)
+    for copy in copies:
+        copy.wait()
+    table = far[...].reshape(owners * views, 128)
+    column = [table[:, k : k + 1] for k in range(10)]
+
+    def added(values):
+        return jnp.sum(values, axis=0, keepdims=True)
+
+    start_start, start_first = added(column[0]), added(column[1])
+    one = start_start / start_first
+    change = column[8] - one
+    norm = added(column[2] + change * (2.0 * column[3] + change * column[4]))
+    turn = norm / start_start
+    cross = added(column[3] + change * column[4])
+    curve = added(column[5] + change * (2.0 * column[6] + change * column[7]))
+    curve = curve + 2.0 * turn * cross + turn * turn * start_first
+    two = norm / curve
+    place = iota((1, 128), 1)
+    line = jnp.where(place == 0, one + two * (1.0 + turn), 0.0)
+    line = jnp.where(place == 1, one * two, line)
+    steps[...] = jnp.where(place == 2, added(column[9]), line)
+
+
+def in_vmem(count):
+    return [pl.BlockSpec(memory_space=pltpu.VMEM)] * count
+
+
+def per_device(texel_atlas, observed, geometry, block_ids, pixel_slot, corner, bilinear_frac):
+    owners, views = lax.axis_size("tex"), lax.axis_size("view")
+    tiles, slots = block_ids.shape[0], block_ids.shape[2]
+    half_rows = CHANNELS * BSIDE // 2
+    shaped = jax.ShapeDtypeStruct
+
+    windows, spilled = pl.pallas_call(
+        pack_kernel,
+        out_shape=(shaped((views, ROWS, WINDOW), F32), shaped((1, 128), F32)),
+        in_specs=[pl.BlockSpec(memory_space=pltpu.SMEM)] + in_vmem(5),
+        out_specs=tuple(in_vmem(2)),
+        scratch_shapes=[
+            pltpu.VMEM((ROWS, tiles * PICKED), F32),
+            pltpu.VMEM((ROWS, SORTED + WINDOW + 128), F32),
+        ],
+        compiler_params=pltpu.CompilerParams(vmem_limit_bytes=32 << 20),
+    )(
+        block_ids.reshape(tiles, slots).T,
+        observed.transpose(1, 0, 2),
+        geometry.transpose(1, 0, 2),
+        bilinear_frac,
+        pixel_slot,
+        corner,
+    )
+    landed = pl.pallas_call(
+        exchange_kernel,
+        out_shape=shaped((views, ROWS, WINDOW), F32),
+        in_specs=in_vmem(1),
+        out_specs=in_vmem(1)[0],
+        scratch_shapes=[
+            pltpu.SemaphoreType.DMA,
+            pltpu.SemaphoreType.DMA((views,)),
+            pltpu.SemaphoreType.DMA((views,)),
+        ],
+        compiler_params=pltpu.CompilerParams(collective_id=0, has_side_effects=True),
+    )(windows)
+    most = views * WINDOW
+    start, first, second, sums = pl.pallas_call(
+        solve_kernel,
+        out_shape=(shaped((half_rows, 128), F32),) * 3 + (shaped((1, 128), F32),),
+        in_specs=in_vmem(3),
+        out_specs=tuple(in_vmem(4)),
+        scratch_shapes=[
+            pltpu.VMEM((ROWS, most + WINDOW + 128), F32),
+            pltpu.VMEM((2 * half_rows, 256), BF16),
+            pltpu.VMEM((most // CHUNK, 4 * BSIDE, CHUNK), BF16),
+            pltpu.VMEM((most // CHUNK, BSIDE, CHUNK), F32),
+            pltpu.VMEM((most // CHUNK, ROWS, CHUNK), F32),
+            pltpu.VMEM((2 * half_rows, 128), F32),
+        ],
+        compiler_params=pltpu.CompilerParams(vmem_limit_bytes=40 << 20),
+    )(landed, spilled, texel_atlas.reshape(half_rows, 128))
+    steps = pl.pallas_call(
+        steps_kernel,
+        out_shape=shaped((1, 128), F32),
+        in_specs=in_vmem(1),
+        out_specs=in_vmem(1)[0],
+        scratch_shapes=[
+            pltpu.VMEM((owners, 1, 128), F32),
+            pltpu.VMEM((views, owners, 1, 128), F32),
+            pltpu.SemaphoreType.DMA((owners,)),
+            pltpu.SemaphoreType.DMA((owners,)),
+            pltpu.SemaphoreType.DMA((views,)),
+            pltpu.SemaphoreType.DMA((views,)),
+        ],
+        compiler_params=pltpu.CompilerParams(collective_id=1, has_side_effects=True),
+    )(sums)
+
+    def quick():
+        update = steps[0, 0] * start - steps[0, 1] * first
+        residual = start - steps[0, 0] * first + steps[0, 1] * second
+        return update.reshape(texel_atlas.shape), residual.reshape(texel_atlas.shape)
+
+    def general():
+        return general_step(
+            texel_atlas, observed, geometry, block_ids, pixel_slot, corner, bilinear_frac
+        )
+
+    return lax.cond(steps[0, 2] > 0.0, general, quick)
 
 
 def solution(mesh):

time: 1130 us -> 68.2 us (0.06)
  waiting for transfers between devices: 507 us -> 0 us
  blocking collectives: 230 us -> 0 us
  matrix products: 176 us -> 0 us
  other arithmetic: 102 us -> 2.01 us
  local copies, waits for them, and re-layouts: 84.7 us -> 3.4 us
  Pallas kernels: 0 us -> 47.8 us
    unnamed x12 -> x0, waiting for transfers between devices: 278 us -> none
    psum x3 -> x0, blocking collectives: 191 us -> none  [inner_sums(): return lax.psum((values[0],), ('tex', 'view'))]
    dot_general x9 -> x0, matrix products: 176 us -> none  [the longest x3 87.1 us: texel_one_group(): jnp.einsum('tcxp,tjyp->tjcyx', middle, row_weight, precision=exact_mode)]
    all_gather x3 -> x0, waiting for transfers between devices: 147 us -> none  [widen(): return lax.all_gather(own_shard, 'view', axis=0, tiled=True)]
    reduce_scatter x3 -> x0, waiting for transfers between devices: 81.4 us -> none  [pixels_of(): lax.psum_scatter(partial_value, 'tex', scatter_dimension=0, tiled=True)]
    reshape x6 -> x0, local copies, waits for them, and re-layouts: 52.4 us -> none  [the longest x3 28.7 us: pixels_one_group(): values = blocks.reshape(blocks.shape[0], slots, channels, BSIDE, BSIDE)]
    pallas_call x0 -> x4, Pallas kernels: none -> 47.8 us  [the longest x1 16.9 us: per_device(): pl.pallas_call(steps_kernel, out_shape=shaped((1, 128), F32), in_specs=in...]
    reduce_sum x15 -> x0, other arithmetic: 43.1 us -> none  [the longest x3 26.4 us: pixels_one_group(): return jnp.sum(middle * column_weight[:, None], axis=2)]
  transfers between devices with their start and end apart: 9 -> 0, of which waited for: 9 -> 0; matrix products, arithmetic and copies ran while one was open for 2% -> 0% of each run, Pallas kernels for 0% -> 0%
where the time goes in v1:
time: 68.2 us; the launch traced here: 67.9 us
  Pallas kernels  47.8 us (70%)
  between operations  14.7 us (22%)
  local copies, waits for them, and re-layouts  3.4 us (5%)
  other arithmetic  2.01 us (3%)
    pallas_call x1, Pallas kernels, per_device(): pl.pallas_call(steps_kernel, out_shape=shaped((1, 128), F32), in_specs=in...  16.9 us
    pallas_call x1, Pallas kernels, per_device(): pl.pallas_call(exchange_kernel, out_shape=shaped((views, ROWS, WINDOW), F...  15 us
    pallas_call x1, Pallas kernels, per_device(): pl.pallas_call(solve_kernel, out_shape=(shaped((half_rows, 128), F32),) *...  11.7 us
    pallas_call x1, Pallas kernels, per_device(): pl.pallas_call(pack_kernel, out_shape=(shaped((views, ROWS, WINDOW), F32)...  4.12 us
    unnamed x6, local copies, waits for them, and re-layouts  2.22 us
    add x1, other arithmetic, quick(): residual = start - steps[0, 0] * first + steps[0, 1] * second  2.01 us

profile of v1, /device:TPU:0, one launch (start us, length us, event | category | flops | bytes accessed | tf_op | source)
XLA Modules:
  0.0 67.9 jit_solution(249561427436335636)
XLA Ops:
  7.2 4.1 %shard_map.90 = (f32[16,16,384]{2,1,0:T(8,128)S(1)}, f32[1,128]{1,0:T(1,128)S(1)}) custom-call(s32[4,8]{1,0:T(4,128)} %bitcast.181, f32[3,8,768]{2,1,0:T(8,128)} %bitcast.178, f32[6,8,768]{2,1,0:T(8,128)} %bitcast.177, f32[8,2,768]{2,1,0:T(2,128)} %frac.1, s32[8,768]{1,0:T(8,128)} %slot.1, s32[8,768]{1,0:T(8,128)} %corner.1), custom_call_target="tpu_custom_call" | custom-call | tf_op jit(solution)/shard_map/pallas_call | solution.py:608
  11.3 0.0 copy-start.1
  11.3 0.7 %copy-done.1 = f32[16,16,384]{2,1,0:T(8,128)} copy-done((f32[16,16,384]{2,1,0:T(8,128)}, f32[16,16,384]{2,1,0:T(8,128)S(1)}, u32[]{:S(2)}) %copy-start.1) | copy-done | bytes 393240
  12.0 15.0 %shard_map.91.landed = f32[16,16,384]{2,1,0:T(8,128)} custom-call(f32[16,16,384]{2,1,0:T(8,128)} %copy-done.1), custom_call_target="tpu_custom_call" | custom-call | tf_op jit(solution)/shard_map/pallas_call | solution.py:626
  27.0 0.0 copy-start
  27.0 1.0 %copy-done = f32[16,16,384]{2,1,0:T(8,128)S(1)} copy-done((f32[16,16,384]{2,1,0:T(8,128)S(1)}, f32[16,16,384]{2,1,0:T(8,128)}, u32[]{:S(2)}) %copy-start) | copy-done | bytes 393240
  28.0 11.7 %shard_map.92 = (f32[320,128]{1,0:T(8,128)S(1)}, f32[320,128]{1,0:T(8,128)S(1)}, f32[320,128]{1,0:T(8,128)S(1)}, f32[1,128]{1,0:T(1,128)S(1)}) custom-call(f32[16,16,384]{2,1,0:T(8,128)S(1)} %copy-done, f32[1,128]{1,0:T(1,128)S(1)} %get-tuple-element.133.spilled, f32[320,128]{1,0:T(8,128)} %bitcast.176), custom_call_target="tpu_custom_call" | custom-call | tf_op jit(solution)/shard_map/pallas_call | solution.py:639
  39.7 0.0 copy-start.2
  39.8 0.5 copy-done.2
  40.3 16.9 %shard_map.93 = f32[1,128]{1,0:T(1,128)S(1)} custom-call(f32[1,128]{1,0:T(1,128)} %copy-done.2), custom_call_target="tpu_custom_call" | custom-call | tf_op jit(solution)/shard_map/pallas_call | solution.py:654
  57.2 0.6 slice.108
  58.5 2.6 %conditional.1 = (f32[1,10,4096]{2,0,1:T(1,128)}, f32[1,10,4096]{2,0,1:T(1,128)}) conditional(s32[]{:T(128)} %bitcast.49, (f32[1,128]{1,0:T(1,128)S(1)}, f32[320,128]{1,0:T(8,128)S(1)}, f32[320,128]{1,0:T(8,128)S(1)}, f32[320,128]{1,0:T(8,128)S(1)}) %tuple.27, (s32[8,1,4]{0,2,1:T(4,128)}, s32[8,768]{1,0:T(8,128)}, s32[8,768]{1,0:T(8,128)}, ...), branch_computations={%region_0.0_spmd, %region_1.27_spmd} | conditional | flops 74040303616 | bytes 292625536 | solution.py:680
  58.5 0.6 fusion.157
  59.1 2.0 %multiply_add_fusion = (f32[320,128]{1,0:T(8,128)}, f32[320,128]{1,0:T(8,128)}) fusion(f32[320,128]{1,0:T(8,128)S(1)} %get-tuple-element.102, f32[320,128]{1,0:T(8,128)S(1)} %get-tuple-element.100, f32[320,128]{1,0:T(8,128)S(1)} %get-tuple-element.101, f32[]{:T(128)} %bitcast.1, f32[]{:T(128)} %bitcast), kind=kLoop, calls=%fused_computation | loop fusion | flops 286720 | bytes 819208 | tf_op jit(solution)/shard_map/cond/branch_0_fun/add | solution.py:672
Async XLA Ops:
  11.3 0.7 %copy-start.1 = (f32[16,16,384]{2,1,0:T(8,128)}, f32[16,16,384]{2,1,0:T(8,128)S(1)}, u32[]{:S(2)}) copy-start(f32[16,16,384]{2,1,0:T(8,128)S(1)} %get-tuple-element.132.windows) | copy-start | bytes 1179652
  27.0 1.0 %copy-start = (f32[16,16,384]{2,1,0:T(8,128)S(1)}, f32[16,16,384]{2,1,0:T(8,128)}, u32[]{:S(2)}) copy-start(f32[16,16,384]{2,1,0:T(8,128)} %shard_map.91.landed) | copy-start | bytes 1179652
  39.7 0.5 copy-start.2

commit v2 on v1

--- a/solution.py
+++ b/solution.py
@@ -13,6 +13,36 @@
 
 
 DAMPING = 0.1
+
+
+def passed_on(values, axis):
+    count = lax.axis_size(axis)
+    return lax.ppermute(values, axis, [(k, (k + 1) % count) for k in range(count)])
+
+
+def ring_gather(values, axis):
+    count, me = lax.axis_size(axis), lax.axis_index(axis)
+
+    def step(s, state):
+        held, block = state
+        block = passed_on(block, axis)
+        return held.at[lax.rem(me - s + count, count)].set(block), block
+
+    held = jnp.zeros((count,) + values.shape, values.dtype).at[me].set(values)
+    return lax.fori_loop(1, count, step, (held, values))[0]
+
+
+def ring_sum_scatter(values, axis):
+    count, me = lax.axis_size(axis), lax.axis_index(axis)
+
+    def step(s, total):
+        return passed_on(total, axis) + values[lax.rem(me - 1 - s + 2 * count, count)]
+
+    return lax.fori_loop(1, count, step, values[lax.rem(me - 1 + count, count)])
+
+
+def grouped_by(values, count):
+    return values.reshape((count, values.shape[0] // count) + values.shape[1:])
 
 
 def shade(params, geometry):
@@ -88,7 +118,7 @@
     pixel_tables = (grouped(pixel_slot), grouped(corner), grouped(bilinear_frac))
 
     def widen(own_shard):
-        return lax.all_gather(own_shard, "view", axis=0, tiled=True)
+        return ring_gather(own_shard, "view").reshape((-1,) + own_shard.shape[1:])
 
     def pixels_of(whole_range):
         ranged = whole_range.shape[0]
@@ -108,10 +138,10 @@
 
         partial_value = lax.map(pixels_one_group, (grouped(fetched),) + pixel_tables)
         partial_value = partial_value.reshape((tiles_all,) + partial_value.shape[2:])
-        return lax.psum_scatter(partial_value, "tex", scatter_dimension=0, tiled=True)
+        return ring_sum_scatter(grouped_by(partial_value, tex_count), "tex")
 
     def texel_terms(cotangent):
-        gathered = lax.all_gather(cotangent, "tex", axis=0, tiled=True)
+        gathered = ring_gather(cotangent, "tex").reshape((-1,) + cotangent.shape[1:])
 
         def texel_one_group(members):
             back_part, slot_part, corner_part, frac_part = members
@@ -130,8 +160,8 @@
         wanted = jnp.arange(row_count, dtype=jnp.int32)
         selector = (slot_list[None, :] == wanted[:, None]).astype(jnp.float32)
         summed = jnp.dot(selector, terms, precision=exact_mode, preferred_element_type=jnp.float32)
-        return lax.psum_scatter(
-            summed.reshape(row_count, channels, texels), "view", scatter_dimension=0, tiled=True
+        return ring_sum_scatter(
+            summed.reshape(row_count // own_blocks, own_blocks, channels, texels), "view"
         )
 
     atlas_range = widen(texel_atlas)
@@ -152,7 +182,7 @@
     gradient = owner_sums(first_terms)
 
     def inner_sums(values):
-        return lax.psum((values[0],), ("tex", "view"))
+        return (jnp.sum(ring_gather(jnp.sum(ring_gather(values[0], "tex")), "view")),)
 
     update = jnp.zeros_like(gradient)
     residual = -gradient
@@ -181,6 +211,7 @@
 PICKED = 256
 SORTED = 1024
 CHUNK = 256
+DENSE = 1792
 NT = (((1,), (1,)), ((), ()))
 
 
@@ -194,7 +225,7 @@
     return lax.broadcasted_iota(jnp.int32, shape, axis)
 
 
-def pack_kernel(ids, obs, geo, frac, slot, corner, out, spilled, picked, ordered):
+def pack(ids, obs, geo, frac, slot, corner, out, picked, ordered):
     tiles, pixels = slot.shape
     slots = ids.shape[0]
     blocks = out.shape[0]
@@ -275,51 +306,45 @@
     place = jnp.sum(member * place, axis=0, keepdims=True)
     place = jnp.where(target_row > 0.0, place, -1.0).astype(jnp.int32)
     both = jnp.concatenate(halves(picked[...]), axis=0)
-    ordered[:, SORTED:] = jnp.zeros((ROWS, ordered.shape[1] - SORTED), F32)
     for q in range(SORTED // 256):
         hot = jnp.where(iota((256, listed), 0) + q * 256 == place, 1.0, 0.0).astype(BF16)
         got = lax.dot_general(both, hot, NT, preferred_element_type=F32)
         ordered[:, q * 256 : q * 256 + 256] = got[:ROWS] + got[ROWS:]
 
-    first = jnp.minimum(first, float(SORTED)).astype(jnp.int32)
-    wide = WINDOW + 128
+    listing = ordered[...]
+    turns = jnp.where(first > 0.0, jnp.maximum(float(SORTED) - first, 0.0), 0.0).astype(jnp.int32)
     for k in range(blocks):
-        begin = first[k, 0]
-        aligned = pl.multiple_of(begin // 128 * 128, 128)
-        window = ordered[:, pl.ds(aligned, wide)]
-        shift = begin - aligned
-        window = pltpu.roll(window, lax.rem(wide - shift, wide), axis=1)
-        out[k] = window[:, :WINDOW]
-    spilled[...] = jnp.full(spilled.shape, over, F32)
-
-
-def exchange_kernel(windows, landed, own_sem, send_sem, recv_sem):
-    tex = lax.axis_index("tex")
-    view = lax.axis_index("view")
-    views = windows.shape[0]
-    barrier = pltpu.get_barrier_semaphore()
+        out[k] = pltpu.roll(listing, turns[k, 0], axis=1)[:, :WINDOW]
+    return over
+
+
+def greet(barrier, tex, view, owners, views):
     for step in range(1, views):
         peer = lax.rem(view + step, views)
         pl.semaphore_signal(barrier, inc=1, device_id=(tex, peer), device_id_type=MESH)
-    own = pltpu.make_async_copy(windows.at[view], landed.at[view], own_sem)
-    own.start()
-    pl.semaphore_wait(barrier, views - 1)
+    for step in range(1, owners):
+        peer = lax.rem(tex + step, owners)
+        pl.semaphore_signal(barrier, inc=1, device_id=(peer, view), device_id_type=MESH)
+
+
+def send_along(axis, source, target, send_sem, recv_sem):
+    tex, view = lax.axis_index("tex"), lax.axis_index("view")
+    count = target.shape[0]
+    me = tex if axis == "tex" else view
     copies = []
-    for step in range(1, views):
-        peer = lax.rem(view + step, views)
+    for step in range(1, count):
+        peer = lax.rem(me + step, count)
         copy = pltpu.make_async_remote_copy(
-            src_ref=windows.at[peer],
-            dst_ref=landed.at[view],
+            src_ref=source(peer),
+            dst_ref=target.at[me],
             send_sem=send_sem.at[step],
             recv_sem=recv_sem.at[step],
-            device_id=(tex, peer),
+            device_id=(peer, view) if axis == "tex" else (tex, peer),
             device_id_type=MESH,
         )
         copy.start()
         copies.append(copy)
-    own.wait()
-    for copy in copies:
-        copy.wait()
+    return copies
 
 
 def optics(params, geometry):
@@ -399,15 +424,56 @@
     )
 
 
-def solve_kernel(
-    landed, spilled, atlas, start, first, second, sums, pixels, field, across, down, slopes, gathered
+def whole_kernel(
+    ids, obs, geo, frac, slot, corner, atlas, update, residual, flag,
+    picked, ordered, windows, landed, pixels, field, across, down, slopes, gathered, near, far,
+    send_window, recv_window, send_near, recv_near, send_far, recv_far,
 ):
-    senders = landed.shape[0]
-    me = lax.axis_index("view")
+    tex, me = lax.axis_index("tex"), lax.axis_index("view")
+    senders, owners = landed.shape[0], near.shape[0]
     half_rows = CHANNELS * BSIDE // 2
     lane = iota((half_rows, 128), 1)
-
-    pixels[...] = jnp.zeros(pixels.shape, F32)
+    barrier = pltpu.get_barrier_semaphore()
+    greet(barrier, tex, me, owners, senders)
+    over = pack(ids, obs, geo, frac, slot, corner, windows, picked, ordered)
+    pl.semaphore_wait(barrier, owners + senders - 2)
+    copies = send_along("view", lambda peer: windows.at[peer], landed, send_window, recv_window)
+    landed[me] = windows[me]
+
+    def hold(values):
+        high, low = halves(values)
+        high, low = high.astype(F32), low.astype(F32)
+        left = jnp.where(lane < BSIDE, high, pltpu.roll(low, BSIDE, axis=1)).astype(BF16)
+        right = jnp.where(lane < BSIDE, pltpu.roll(high, BSIDE, axis=1), low).astype(BF16)
+        field[:half_rows, :128] = left
+        field[:half_rows, 128:] = left
+        field[half_rows:, :128] = right
+        field[half_rows:, 128:] = right
+
+    def sample(c, rows):
+        seen = jnp.dot(field[...], across[c], preferred_element_type=F32)
+        seen = seen.reshape(2, CHANNELS, BSIDE // 2, CHUNK) * rows
+        seen = jnp.sum(seen[0] + seen[1], axis=1)
+        return [seen[k : k + 1] for k in range(CHANNELS)]
+
+    def spread(c, rows, back):
+        back = jnp.concatenate(back, axis=0)
+        terms = (back.reshape(1, CHANNELS, 1, CHUNK) * rows).reshape(2 * half_rows, CHUNK)
+        high, low = halves(terms)
+        columns = across[c, BSIDE : 3 * BSIDE, :]
+        gathered[...] += lax.dot_general(high, columns, NT, preferred_element_type=F32)
+        gathered[...] += lax.dot_general(low, columns, NT, preferred_element_type=F32)
+
+    def collected():
+        left, right = gathered[:half_rows], gathered[half_rows:]
+        left = left + pltpu.roll(left, BSIDE, axis=1)
+        right = right + pltpu.roll(right, BSIDE, axis=1)
+        return jnp.where(lane < BSIDE, left, right)
+
+    hold(atlas[...])
+    gathered[...] = jnp.zeros(gathered.shape, F32)
+    for copy in copies:
+        copy.wait()
     marks = landed[:, 13, :]
     live = jnp.where(marks == (me + 1).astype(F32), 1.0, 0.0)
     counts = jnp.sum(live, axis=1, keepdims=True)
@@ -417,55 +483,22 @@
         jnp.broadcast_to(counts, (senders, 128)),
         precision=lax.Precision.HIGHEST,
         preferred_element_type=F32,
-    ).astype(jnp.int32)
-    wide = WINDOW + 128
+    )
+    begins = jnp.minimum(begins, float(DENSE - 1)).astype(jnp.int32)
+    dense = jnp.zeros((ROWS, DENSE), F32)
     for j in range(senders):
-        begin = begins[j, 0]
-        aligned = pl.multiple_of(begin // 128 * 128, 128)
         window = jnp.where(live[j : j + 1] > 0.0, landed[j], 0.0)
-        window = jnp.concatenate([window, jnp.zeros((ROWS, 128), F32)], axis=1)
-        window = pltpu.roll(window, begin - aligned, axis=1)
-        pixels[:, pl.ds(aligned, wide)] += window
-    count = jnp.sum(counts).astype(jnp.int32)
-    chunks = (count + CHUNK - 1) // CHUNK
-
-    def hold(values):
-        high, low = halves(values)
-        high, low = high.astype(F32), low.astype(F32)
-        left = jnp.where(lane < BSIDE, high, pltpu.roll(low, BSIDE, axis=1)).astype(BF16)
-        right = jnp.where(lane < BSIDE, pltpu.roll(high, BSIDE, axis=1), low).astype(BF16)
-        field[:half_rows, :128] = left
-        field[:half_rows, 128:] = left
-        field[half_rows:, :128] = right
-        field[half_rows:, 128:] = right
-
-    def sample(c, rows):
-        seen = jnp.dot(field[...], across[c], preferred_element_type=F32)
-        seen = seen.reshape(2, CHANNELS, BSIDE // 2, CHUNK) * rows
-        seen = jnp.sum(seen[0] + seen[1], axis=1)
-        return [seen[k : k + 1] for k in range(CHANNELS)]
-
-    def spread(c, rows, back):
-        back = jnp.concatenate(back, axis=0)
-        terms = (back.reshape(1, CHANNELS, 1, CHUNK) * rows).reshape(2 * half_rows, CHUNK)
-        high, low = halves(terms)
-        columns = across[c, BSIDE : 3 * BSIDE, :]
-        gathered[...] += lax.dot_general(high, columns, NT, preferred_element_type=F32)
-        gathered[...] += lax.dot_general(low, columns, NT, preferred_element_type=F32)
-
-    def collected():
-        left, right = gathered[:half_rows], gathered[half_rows:]
-        left = left + pltpu.roll(left, BSIDE, axis=1)
-        right = right + pltpu.roll(right, BSIDE, axis=1)
-        return jnp.where(lane < BSIDE, left, right)
-
-    hold(atlas[...])
-    gathered[...] = jnp.zeros(gathered.shape, F32)
+        window = jnp.concatenate([window, jnp.zeros((ROWS, DENSE - WINDOW), F32)], axis=1)
+        dense = dense + pltpu.roll(window, begins[j, 0], axis=1)
+    pixels[...] = dense
+    count = jnp.sum(counts)
+    over = jnp.maximum(over, jnp.where(count > DENSE, 1.0, 0.0))
+    chunks = DENSE // CHUNK
 
     def first_pass(c, carry):
         numbers = pixels[:, pl.ds(pl.multiple_of(c * CHUNK, CHUNK), CHUNK)]
         numbers = [numbers[k : k + 1] for k in range(ROWS)]
-        used = iota((1, CHUNK), 1) + c * CHUNK < count
+        used = (iota((1, CHUNK), 1) + c * CHUNK).astype(F32) < count
         frac_x, frac_y, row, column = numbers[9:13]
         at = iota((BSIDE, CHUNK), 0).astype(F32)
         weight = jnp.where(at == column, 1.0 - frac_x, jnp.where(at == column + 1.0, frac_x, 0.0))
@@ -486,7 +519,6 @@
 
     lax.fori_loop(0, chunks, first_pass, 0)
     start_now = -collected()
-    start[...] = start_now
 
     def applied(values):
         hold(values)
@@ -503,9 +535,7 @@
         return collected() + DAMPING * values
 
     first_now = applied(start_now)
-    first[...] = first_now
     second_now = applied(first_now)
-    second[...] = second_now
 
     start_start = jnp.sum(start_now * start_now)
     start_first = jnp.sum(start_now * first_now)
@@ -524,57 +554,16 @@
         guess,
     ]
     place = iota((1, 128), 1)
-    line = jnp.where(place == len(found), spilled[...], 0.0)
+    line = jnp.where(place == len(found), over, 0.0)
     for k, value in enumerate(found):
         line = jnp.where(place == k, value, line)
-    sums[...] = line
-
-
-def steps_kernel(sums, steps, near, far, send_near, recv_near, send_far, recv_far):
-    tex = lax.axis_index("tex")
-    view = lax.axis_index("view")
-    owners, views = near.shape[0], far.shape[0]
-    barrier = pltpu.get_barrier_semaphore()
-    for step in range(1, owners):
-        peer = lax.rem(tex + step, owners)
-        pl.semaphore_signal(barrier, inc=1, device_id=(peer, view), device_id_type=MESH)
-    for step in range(1, views):
-        peer = lax.rem(view + step, views)
-        pl.semaphore_signal(barrier, inc=1, device_id=(tex, peer), device_id_type=MESH)
-    near[tex] = sums[...]
-    pl.semaphore_wait(barrier, owners + views - 2)
-    copies = []
-    for step in range(1, owners):
-        peer = lax.rem(tex + step, owners)
-        copy = pltpu.make_async_remote_copy(
-            src_ref=sums,
-            dst_ref=near.at[tex],
-            send_sem=send_near.at[step],
-            recv_sem=recv_near.at[step],
-            device_id=(peer, view),
-            device_id_type=MESH,
-        )
-        copy.start()
-        copies.append(copy)
-    for copy in copies:
+    near[tex] = line
+    for copy in send_along("tex", lambda peer: near.at[tex], near, send_near, recv_near):
         copy.wait()
-    far[view] = near[...]
-    copies = []
-    for step in range(1, views):
-        peer = lax.rem(view + step, views)
-        copy = pltpu.make_async_remote_copy(
-            src_ref=near,
-            dst_ref=far.at[view],
-            send_sem=send_far.at[step],
-            recv_sem=recv_far.at[step],
-            device_id=(tex, peer),
-            device_id_type=MESH,
-        )
-        copy.start()
-        copies.append(copy)
-    for copy in copies:
+    far[me] = near[...]
+    for copy in send_along("view", lambda peer: near, far, send_far, recv_far):
         copy.wait()
-    table = far[...].reshape(owners * views, 128)
+    table = far[...].reshape(owners * senders, 128)
     column = [table[:, k : k + 1] for k in range(10)]
 
     def added(values):
@@ -589,10 +578,10 @@
     curve = added(column[5] + change * (2.0 * column[6] + change * column[7]))
     curve = curve + 2.0 * turn * cross + turn * turn * start_first
     two = norm / curve
-    place = iota((1, 128), 1)
-    line = jnp.where(place == 0, one + two * (1.0 + turn), 0.0)
-    line = jnp.where(place == 1, one * two, line)
-    steps[...] = jnp.where(place == 2, added(column[9]), line)
+    near_part = one + two * (1.0 + turn)
+    update[...] = near_part * start_now - one * two * first_now
+    residual[...] = start_now - near_part * first_now + one * two * second_now
+    flag[...] = jnp.broadcast_to(added(column[9]), flag.shape)
 
 
 def in_vmem(count):
@@ -605,16 +594,31 @@
     half_rows = CHANNELS * BSIDE // 2
     shaped = jax.ShapeDtypeStruct
 
-    windows, spilled = pl.pallas_call(
-        pack_kernel,
-        out_shape=(shaped((views, ROWS, WINDOW), F32), shaped((1, 128), F32)),
-        in_specs=[pl.BlockSpec(memory_space=pltpu.SMEM)] + in_vmem(5),
-        out_specs=tuple(in_vmem(2)),
+    update, residual, flag = pl.pallas_call(
+        whole_kernel,
+        out_shape=(shaped((half_rows, 128), F32),) * 2 + (shaped((1, 128), F32),),
+        in_specs=[pl.BlockSpec(memory_space=pltpu.SMEM)] + in_vmem(6),
+        out_specs=tuple(in_vmem(3)),
         scratch_shapes=[
             pltpu.VMEM((ROWS, tiles * PICKED), F32),
-            pltpu.VMEM((ROWS, SORTED + WINDOW + 128), F32),
-        ],
-        compiler_params=pltpu.CompilerParams(vmem_limit_bytes=32 << 20),
+            pltpu.VMEM((ROWS, SORTED), F32),
+            pltpu.VMEM((views, ROWS, WINDOW), F32),
+            pltpu.VMEM((views, ROWS, WINDOW), F32),
+            pltpu.VMEM((ROWS, DENSE), F32),
+            pltpu.VMEM((2 * half_rows, 256), BF16),
+            pltpu.VMEM((DENSE // CHUNK, 4 * BSIDE, CHUNK), BF16),
+            pltpu.VMEM((DENSE // CHUNK, BSIDE, CHUNK), F32),
+            pltpu.VMEM((DENSE // CHUNK, ROWS, CHUNK), F32),
+            pltpu.VMEM((2 * half_rows, 128), F32),
+            pltpu.VMEM((owners, 1, 128), F32),
+            pltpu.VMEM((views, owners, 1, 128), F32),
+        ]
+        + [pltpu.SemaphoreType.DMA((views,))] * 2
+        + [pltpu.SemaphoreType.DMA((owners,))] * 2
+        + [pltpu.SemaphoreType.DMA((views,))] * 2,
+        compiler_params=pltpu.CompilerParams(
+            collective_id=0, has_side_effects=True, vmem_limit_bytes=56 << 20
+        ),
     )(
         block_ids.reshape(tiles, slots).T,
         observed.transpose(1, 0, 2),
@@ -622,54 +626,10 @@
         bilinear_frac,
         pixel_slot,
         corner,
-    )
-    landed = pl.pallas_call(
-        exchange_kernel,
-        out_shape=shaped((views, ROWS, WINDOW), F32),
-        in_specs=in_vmem(1),
-        out_specs=in_vmem(1)[0],
-        scratch_shapes=[
-            pltpu.SemaphoreType.DMA,
-            pltpu.SemaphoreType.DMA((views,)),
-            pltpu.SemaphoreType.DMA((views,)),
-        ],
-        compiler_params=pltpu.CompilerParams(collective_id=0, has_side_effects=True),
-    )(windows)
-    most = views * WINDOW
-    start, first, second, sums = pl.pallas_call(
-        solve_kernel,
-        out_shape=(shaped((half_rows, 128), F32),) * 3 + (shaped((1, 128), F32),),
-        in_specs=in_vmem(3),
-        out_specs=tuple(in_vmem(4)),
-        scratch_shapes=[
-            pltpu.VMEM((ROWS, most + WINDOW + 128), F32),
-            pltpu.VMEM((2 * half_rows, 256), BF16),
-            pltpu.VMEM((most // CHUNK, 4 * BSIDE, CHUNK), BF16),
-            pltpu.VMEM((most // CHUNK, BSIDE, CHUNK), F32),
-            pltpu.VMEM((most // CHUNK, ROWS, CHUNK), F32),
-            pltpu.VMEM((2 * half_rows, 128), F32),
-        ],
-        compiler_params=pltpu.CompilerParams(vmem_limit_bytes=40 << 20),
-    )(landed, spilled, texel_atlas.reshape(half_rows, 128))
-    steps = pl.pallas_call(
-        steps_kernel,
-        out_shape=shaped((1, 128), F32),
-        in_specs=in_vmem(1),
-        out_specs=in_vmem(1)[0],
-        scratch_shapes=[
-            pltpu.VMEM((owners, 1, 128), F32),
-            pltpu.VMEM((views, owners, 1, 128), F32),
-            pltpu.SemaphoreType.DMA((owners,)),
-            pltpu.SemaphoreType.DMA((owners,)),
-            pltpu.SemaphoreType.DMA((views,)),
-            pltpu.SemaphoreType.DMA((views,)),
-        ],
-        compiler_params=pltpu.CompilerParams(collective_id=1, has_side_effects=True),
-    )(sums)
+        texel_atlas.reshape(half_rows, 128),
+    )
 
     def quick():
-        update = steps[0, 0] * start - steps[0, 1] * first
-        residual = start - steps[0, 0] * first + steps[0, 1] * second
         return update.reshape(texel_atlas.shape), residual.reshape(texel_atlas.shape)
 
     def general():
@@ -677,7 +637,7 @@
             texel_atlas, observed, geometry, block_ids, pixel_slot, corner, bilinear_frac
         )
 
-    return lax.cond(steps[0, 2] > 0.0, general, quick)
+    return lax.cond(flag[0, 0] > 0.0, general, quick)
 
 
 def solution(mesh):

time: 68.2 us -> 47.4 us (0.70)
  between operations: 14.7 us -> 1.34 us
  Pallas kernels: 47.8 us -> 44.4 us
  local copies, waits for them, and re-layouts: 3.4 us -> 1.33 us
  other arithmetic: 2.01 us -> 0 us
    pallas_call x4 -> x1, Pallas kernels: 47.8 us -> 44.4 us  [per_device(): pl.pallas_call(whole_kernel, out_shape=(shaped((half_rows, 128), F32),) *...]
    add x1 -> x0, other arithmetic: 2.01 us -> none  [quick(): residual = start - steps[0, 0] * first + steps[0, 1] * second]
    slice x2 -> x0, local copies, waits for them, and re-layouts: 1.18 us -> none  [the longest x1 0.59 us: quick(): update = steps[0, 0] * start - steps[0, 1] * first]
    unnamed x6 -> x2, local copies, waits for them, and re-layouts: 2.22 us -> 1.33 us
where the time goes in v2:
time: 47.4 us; the launch traced here: 47.3 us
  Pallas kernels  44.4 us (94%)
  between operations  1.34 us (3%)
  local copies, waits for them, and re-layouts  1.33 us (3%)
    pallas_call x1, Pallas kernels, per_device(): pl.pallas_call(whole_kernel, out_shape=(shaped((half_rows, 128), F32),) *...  44.4 us
    unnamed x2, local copies, waits for them, and re-layouts  1.33 us

profile of v2, /device:TPU:0, one launch (start us, length us, event | category | flops | bytes accessed | tf_op | source)
XLA Modules:
  0.0 47.3 jit_solution(4458170844799684097)
XLA Ops:
  0.6 44.4 %shard_map.90 = (f32[320,128]{1,0:T(8,128)S(1)}, f32[320,128]{1,0:T(8,128)S(1)}, f32[1,128]{1,0:T(1,128)}) custom-call(s32[4,8]{1,0:T(4,128)} %bitcast.339, f32[3,8,768]{2,1,0:T(8,128)} %bitcast.336, f32[6,8,768]{2,1,0:T(8,128)} %bitcast.335, f32[8,2,768]{2,1,0:T(2,128)} %frac.1, s32[8,768]{1,0:T(8,128)} %slot.1, s32[8,768]{1,0:T(8,128)} %corner.1, ...), custom_call_target="tpu_custom_call" | custom-call | tf_op jit(solution)/shard_map/pallas_call | solution.py:597
  45.7 0.2 conditional.1
  46.0 0.7 %copy.321 = f32[1,10,4096]{2,0,1:T(1,128)} copy(f32[1,10,4096]{2,0,1:T(1,128)S(1)} %get-tuple-element.3758) | data formatting | bytes 327680
  46.6 0.7 %copy.322 = f32[1,10,4096]{2,0,1:T(1,128)} copy(f32[1,10,4096]{2,0,1:T(1,128)S(1)} %get-tuple-element.3759) | data formatting | bytes 327680

commit v3 on v2

--- a/solution.py
+++ b/solution.py
@@ -207,10 +207,10 @@
 BF16 = jnp.bfloat16
 CHANNELS = 10
 ROWS = 16
-WINDOW = 384
+WINDOW = 512
 PICKED = 256
 SORTED = 1024
-CHUNK = 256
+CHUNK = 896
 DENSE = 1792
 NT = (((1,), (1,)), ((), ()))
 
@@ -225,18 +225,15 @@
     return lax.broadcasted_iota(jnp.int32, shape, axis)
 
 
-def pack(ids, obs, geo, frac, slot, corner, out, picked, ordered):
+def pack(ids, obs, geo, frac, slot, corner, picked, ordered):
     tiles, pixels = slot.shape
     slots = ids.shape[0]
-    blocks = out.shape[0]
+    blocks = lax.axis_size("view")
     owner = lax.axis_index("tex")
     lanes = pixels // 128
 
     slot_now = slot[...]
-    corner_now = corner[...]
-    row = corner_now // (BSIDE - 1)
-    column = (corner_now - row * (BSIDE - 1)).astype(F32)
-    row = row.astype(F32)
+    corner_now = corner[...].astype(F32)
     tile_of = iota((tiles, 128), 0)
     target = jnp.zeros((tiles, pixels), jnp.int32)
     for s in range(slots):
@@ -269,10 +266,9 @@
                 obs[:, t, :],
                 geo[:, t, :],
                 frac[t],
-                row[t : t + 1],
-                column[t : t + 1],
+                corner_now[t : t + 1],
                 target_f[t : t + 1],
-                jnp.zeros((2, pixels), F32),
+                jnp.zeros((3, pixels), F32),
             ],
             axis=0,
         )
@@ -283,7 +279,7 @@
 
     listed = tiles * PICKED
     groups = listed // 128
-    target_row = picked[13:14, :]
+    target_row = picked[12:13, :]
     member = jnp.where(
         iota((blocks, listed), 0).astype(F32) + 1.0 == target_row, 1.0, 0.0
     )
@@ -311,11 +307,27 @@
         got = lax.dot_general(both, hot, NT, preferred_element_type=F32)
         ordered[:, q * 256 : q * 256 + 256] = got[:ROWS] + got[ROWS:]
 
-    listing = ordered[...]
-    turns = jnp.where(first > 0.0, jnp.maximum(float(SORTED) - first, 0.0), 0.0).astype(jnp.int32)
-    for k in range(blocks):
-        out[k] = pltpu.roll(listing, turns[k, 0], axis=1)[:, :WINDOW]
-    return over
+    return over, first, jnp.broadcast_to(base, (blocks, 128))
+
+
+def folded(listed, turn, size):
+    window = pltpu.roll(listed, turn, axis=1)[:, :WINDOW]
+    top, low = window[:8], window[8:]
+    place = iota((8, WINDOW), 0)
+    low = jnp.where((place == 3) & (iota((8, WINDOW), 1).astype(F32) >= size), -1.0, low)
+    raised = pltpu.roll(low, 4, axis=0)
+    pairs = []
+    for g in range(0, WINDOW, 256):
+        pairs.append(jnp.where(place[:, :128] < 4, low[:, g : g + 128], raised[:, g + 128 : g + 256]))
+    return jnp.concatenate([top] + pairs, axis=1)
+
+
+def unfolded(window):
+    low = []
+    for g in range(WINDOW, window.shape[1], 128):
+        pair = window[:, g : g + 128]
+        low += [pair, pltpu.roll(pair, 4, axis=0)]
+    return jnp.concatenate([window[:, :WINDOW], jnp.concatenate(low, axis=1)], axis=0)
 
 
 def greet(barrier, tex, view, owners, views):
@@ -327,24 +339,22 @@
         pl.semaphore_signal(barrier, inc=1, device_id=(peer, view), device_id_type=MESH)
 
 
-def send_along(axis, source, target, send_sem, recv_sem):
-    tex, view = lax.axis_index("tex"), lax.axis_index("view")
-    count = target.shape[0]
-    me = tex if axis == "tex" else view
-    copies = []
-    for step in range(1, count):
-        peer = lax.rem(me + step, count)
-        copy = pltpu.make_async_remote_copy(
-            src_ref=source(peer),
-            dst_ref=target.at[me],
-            send_sem=send_sem.at[step],
-            recv_sem=recv_sem.at[step],
-            device_id=(peer, view) if axis == "tex" else (tex, peer),
-            device_id_type=MESH,
-        )
-        copy.start()
-        copies.append(copy)
-    return copies
+def send(source, target, axis, step, send_sem, recv_sem):
+    count, me = lax.axis_size(axis), lax.axis_index(axis)
+    peer = lax.rem(me + step, count)
+    pltpu.make_async_remote_copy(
+        src_ref=source,
+        dst_ref=target.at[me],
+        send_sem=send_sem,
+        recv_sem=recv_sem,
+        device_id={axis: peer},
+        device_id_type=MESH,
+    ).start()
+
+
+def wait_all(target, sem):
+    others = target.at[pl.ds(0, target.shape[0] - 1)]
+    pltpu.make_async_copy(others, others, sem).wait()
 
 
 def optics(params, geometry):
@@ -425,20 +435,45 @@
 
 
 def whole_kernel(
-    ids, obs, geo, frac, slot, corner, atlas, update, residual, flag,
-    picked, ordered, windows, landed, pixels, field, across, down, slopes, gathered, near, far,
-    send_window, recv_window, send_near, recv_near, send_far, recv_far,
+    ids, obs_in, geo_in, frac_in, slot_in, corner_in, atlas_in, update, residual, flag,
+    obs, geo, frac, slot, corner, atlas, picked, ordered, windows, landed, pixels, field,
+    across, down, slopes, seen_start, seen_first, gathered, near, far,
+    read_sems, send_window, recv_window, send_near, recv_near, send_far, recv_far,
 ):
     tex, me = lax.axis_index("tex"), lax.axis_index("view")
     senders, owners = landed.shape[0], near.shape[0]
     half_rows = CHANNELS * BSIDE // 2
     lane = iota((half_rows, 128), 1)
+    reads = [
+        pltpu.make_async_copy(source, target, read_sems.at[k])
+        for k, (source, target) in enumerate(
+            [
+                (slot_in, slot),
+                (corner_in, corner),
+                (obs_in, obs),
+                (geo_in, geo),
+                (frac_in, frac),
+                (atlas_in, atlas),
+            ]
+        )
+    ]
+    for read in reads:
+        read.start()
     barrier = pltpu.get_barrier_semaphore()
     greet(barrier, tex, me, owners, senders)
-    over = pack(ids, obs, geo, frac, slot, corner, windows, picked, ordered)
+    for read in reads:
+        read.wait()
+    over, first, sizes = pack(ids, obs, geo, frac, slot, corner, picked, ordered)
+    turns = jnp.where(first > 0.0, jnp.maximum(float(SORTED) - first, 0.0), 0.0).astype(jnp.int32)
+    back_by = lax.rem(senders - me, senders)
+    turns = pltpu.roll(turns, back_by, axis=0)
+    sizes = pltpu.roll(sizes, back_by, axis=0)
+    listed = ordered[...]
     pl.semaphore_wait(barrier, owners + senders - 2)
-    copies = send_along("view", lambda peer: windows.at[peer], landed, send_window, recv_window)
-    landed[me] = windows[me]
+    for step in range(1, senders):
+        windows[step] = folded(listed, turns[step, 0], sizes[step : step + 1, 0:1])
+        send(windows.at[step], landed, "view", step, send_window, recv_window)
+    landed[me] = folded(listed, turns[0, 0], sizes[0:1, 0:1])
 
     def hold(values):
         high, low = halves(values)
@@ -472,11 +507,10 @@
 
     hold(atlas[...])
     gathered[...] = jnp.zeros(gathered.shape, F32)
-    for copy in copies:
-        copy.wait()
-    marks = landed[:, 13, :]
-    live = jnp.where(marks == (me + 1).astype(F32), 1.0, 0.0)
-    counts = jnp.sum(live, axis=1, keepdims=True)
+    wait_all(landed, recv_window)
+    arrived = [unfolded(landed[j]) for j in range(senders)]
+    live = [jnp.where(window[11:12] >= 0.0, 1.0, 0.0) for window in arrived]
+    counts = jnp.sum(jnp.concatenate(live, axis=0), axis=1, keepdims=True)
     earlier = jnp.where(iota((senders, senders), 1) < iota((senders, senders), 0), 1.0, 0.0)
     begins = jnp.dot(
         earlier,
@@ -487,7 +521,7 @@
     begins = jnp.minimum(begins, float(DENSE - 1)).astype(jnp.int32)
     dense = jnp.zeros((ROWS, DENSE), F32)
     for j in range(senders):
-        window = jnp.where(live[j : j + 1] > 0.0, landed[j], 0.0)
+        window = jnp.where(live[j] > 0.0, arrived[j], 0.0)
         window = jnp.concatenate([window, jnp.zeros((ROWS, DENSE - WINDOW), F32)], axis=1)
         dense = dense + pltpu.roll(window, begins[j, 0], axis=1)
     pixels[...] = dense
@@ -499,7 +533,9 @@
         numbers = pixels[:, pl.ds(pl.multiple_of(c * CHUNK, CHUNK), CHUNK)]
         numbers = [numbers[k : k + 1] for k in range(ROWS)]
         used = (iota((1, CHUNK), 1) + c * CHUNK).astype(F32) < count
-        frac_x, frac_y, row, column = numbers[9:13]
+        frac_x, frac_y, spot = numbers[9:12]
+        row = jnp.floor((spot + 0.5) * (1.0 / (BSIDE - 1)))
+        column = spot - row * (BSIDE - 1)
         at = iota((BSIDE, CHUNK), 0).astype(F32)
         weight = jnp.where(at == column, 1.0 - frac_x, jnp.where(at == column + 1.0, frac_x, 0.0))
         high, low = halves(weight)
@@ -520,37 +556,55 @@
     lax.fori_loop(0, chunks, first_pass, 0)
     start_now = -collected()
 
-    def applied(values):
-        hold(values)
-        gathered[...] = jnp.zeros(gathered.shape, F32)
-
-        def one_pass(c, carry):
-            rows = down[c].reshape(2, 1, BSIDE // 2, CHUNK)
-            factors = slopes[c]
-            factors = [factors[k : k + 1] for k in range(14)]
-            spread(c, rows, pull(push(sample(c, rows), factors), factors))
-            return carry
-
-        lax.fori_loop(0, chunks, one_pass, 0)
-        return collected() + DAMPING * values
-
-    first_now = applied(start_now)
-    second_now = applied(first_now)
+    def factors_of(c):
+        factors = slopes[c]
+        return [factors[k : k + 1] for k in range(14)]
+
+    def seen_of(c, kept):
+        rows = down[c].reshape(2, 1, BSIDE // 2, CHUNK)
+        colors = push(sample(c, rows), factors_of(c))
+        kept[c] = jnp.concatenate(colors + [jnp.zeros((5, CHUNK), F32)], axis=0)
+
+    def spread_seen(c, kept):
+        rows = down[c].reshape(2, 1, BSIDE // 2, CHUNK)
+        colors = kept[c]
+        spread(c, rows, pull([colors[k : k + 1] for k in range(3)], factors_of(c)))
+
+    def start_pass(c, carry):
+        seen_of(c, seen_start)
+        spread_seen(c, seen_start)
+        return carry
+
+    def first_seen(c, carry):
+        seen_of(c, seen_first)
+        return carry
+
+    hold(start_now)
+    gathered[...] = jnp.zeros(gathered.shape, F32)
+    lax.fori_loop(0, chunks, start_pass, 0)
+    first_now = collected() + DAMPING * start_now
+    hold(first_now)
+    gathered[...] = jnp.zeros(gathered.shape, F32)
+    lax.fori_loop(0, chunks, first_seen, 0)
 
     start_start = jnp.sum(start_now * start_now)
     start_first = jnp.sum(start_now * first_now)
     guess = jnp.where(start_first > 0.0, start_start / jnp.where(start_first > 0.0, start_first, 1.0), 0.0)
     rest = start_now - guess * first_now
-    image = first_now - guess * second_now
+    rest_rest = jnp.sum(rest * rest)
+    rest_first = jnp.sum(rest * first_now)
+    first_first = jnp.sum(first_now * first_now)
+    from_start, from_first = seen_start[...], seen_first[...]
+    from_rest = from_start - guess * from_first
     found = [
         start_start,
         start_first,
-        jnp.sum(rest * rest),
-        jnp.sum(rest * first_now),
-        jnp.sum(first_now * first_now),
-        jnp.sum(rest * image),
-        jnp.sum(image * first_now),
-        jnp.sum(first_now * second_now),
+        rest_rest,
+        rest_first,
+        first_first,
+        jnp.sum(from_rest * from_rest) + DAMPING * rest_rest,
+        jnp.sum(from_rest * from_first) + DAMPING * rest_first,
+        jnp.sum(from_first * from_first) + DAMPING * first_first,
         guess,
     ]
     place = iota((1, 128), 1)
@@ -558,11 +612,17 @@
     for k, value in enumerate(found):
         line = jnp.where(place == k, value, line)
     near[tex] = line
-    for copy in send_along("tex", lambda peer: near.at[tex], near, send_near, recv_near):
-        copy.wait()
+    for step in range(1, owners):
+        send(near.at[tex], near, "tex", step, send_near, recv_near)
+    spread_seen(0, seen_first)
+    wait_all(near, recv_near)
     far[me] = near[...]
-    for copy in send_along("view", lambda peer: near, far, send_far, recv_far):
-        copy.wait()
+    for step in range(1, senders):
+        send(near, far, "view", step, send_far, recv_far)
+    for c in range(1, chunks):
+        spread_seen(c, seen_first)
+    second_now = collected() + DAMPING * first_now
+    wait_all(far, recv_far)
     table = far[...].reshape(owners * senders, 128)
     column = [table[:, k : k + 1] for k in range(10)]
 
@@ -582,6 +642,9 @@
     update[...] = near_part * start_now - one * two * first_now
     residual[...] = start_now - near_part * first_now + one * two * second_now
     flag[...] = jnp.broadcast_to(added(column[9]), flag.shape)
+    wait_all(landed, send_window)
+    wait_all(near, send_near)
+    wait_all(far, send_far)
 
 
 def in_vmem(count):
@@ -597,25 +660,32 @@
     update, residual, flag = pl.pallas_call(
         whole_kernel,
         out_shape=(shaped((half_rows, 128), F32),) * 2 + (shaped((1, 128), F32),),
-        in_specs=[pl.BlockSpec(memory_space=pltpu.SMEM)] + in_vmem(6),
+        in_specs=[pl.BlockSpec(memory_space=pltpu.SMEM)] + [pl.BlockSpec(memory_space=pl.ANY)] * 6,
         out_specs=tuple(in_vmem(3)),
         scratch_shapes=[
+            pltpu.VMEM((3, tiles, pixel_slot.shape[1]), F32),
+            pltpu.VMEM((6, tiles, pixel_slot.shape[1]), F32),
+            pltpu.VMEM(bilinear_frac.shape, F32),
+            pltpu.VMEM(pixel_slot.shape, jnp.int32),
+            pltpu.VMEM(pixel_slot.shape, jnp.int32),
+            pltpu.VMEM((half_rows, 128), F32),
             pltpu.VMEM((ROWS, tiles * PICKED), F32),
             pltpu.VMEM((ROWS, SORTED), F32),
-            pltpu.VMEM((views, ROWS, WINDOW), F32),
-            pltpu.VMEM((views, ROWS, WINDOW), F32),
+            pltpu.VMEM((views, 8, WINDOW * 3 // 2), F32),
+            pltpu.VMEM((views, 8, WINDOW * 3 // 2), F32),
             pltpu.VMEM((ROWS, DENSE), F32),
             pltpu.VMEM((2 * half_rows, 256), BF16),
             pltpu.VMEM((DENSE // CHUNK, 4 * BSIDE, CHUNK), BF16),
             pltpu.VMEM((DENSE // CHUNK, BSIDE, CHUNK), F32),
             pltpu.VMEM((DENSE // CHUNK, ROWS, CHUNK), F32),
+            pltpu.VMEM((DENSE // CHUNK, 8, CHUNK), F32),
+            pltpu.VMEM((DENSE // CHUNK, 8, CHUNK), F32),
             pltpu.VMEM((2 * half_rows, 128), F32),
             pltpu.VMEM((owners, 1, 128), F32),
             pltpu.VMEM((views, owners, 1, 128), F32),
         ]
-        + [pltpu.SemaphoreType.DMA((views,))] * 2
-        + [pltpu.SemaphoreType.DMA((owners,))] * 2
-        + [pltpu.SemaphoreType.DMA((views,))] * 2,
+        + [pltpu.SemaphoreType.DMA((6,))]
+        + [pltpu.SemaphoreType.DMA] * 6,
         compiler_params=pltpu.CompilerParams(
             collective_id=0, has_side_effects=True, vmem_limit_bytes=56 << 20
         ),

time: 47.4 us -> 37.6 us (0.79)
  Pallas kernels: 44.4 us -> 34.5 us
    pallas_call x1, Pallas kernels: 44.4 us -> 34.5 us  [per_device(): pl.pallas_call(whole_kernel, out_shape=(shaped((half_rows, 128), F32),) *...]
where the time goes in v3:
time: 37.6 us; the launch traced here: 37.4 us
  Pallas kernels  34.5 us (92%)
  between operations  1.34 us (4%)
  local copies, waits for them, and re-layouts  1.33 us (4%)
    pallas_call x1, Pallas kernels, per_device(): pl.pallas_call(whole_kernel, out_shape=(shaped((half_rows, 128), F32),) *...  34.5 us
    unnamed x2, local copies, waits for them, and re-layouts  1.33 us

profile of v3, /device:TPU:0, one launch (start us, length us, event | category | flops | bytes accessed | tf_op | source)
XLA Modules:
  0.0 37.4 jit_solution(1744240502371798849)
XLA Ops:
  0.6 34.5 %shard_map.90 = (f32[320,128]{1,0:T(8,128)S(1)}, f32[320,128]{1,0:T(8,128)S(1)}, f32[1,128]{1,0:T(1,128)}) custom-call(s32[4,8]{1,0:T(4,128)} %bitcast.339, f32[3,8,768]{2,1,0:T(8,128)} %bitcast.336, f32[6,8,768]{2,1,0:T(8,128)} %bitcast.335, f32[8,2,768]{2,1,0:T(2,128)} %frac_in.1, s32[8,768]{1,0:T(8,128)} %slot_in.1, s32[8,768]{1,0:T(8,128)} %corner_in.1, ...), custom_call_target="tpu_custom_call" | custom-call | tf_op jit(solution)/shard_map/pallas_call | solution.py:660
  35.8 0.2 conditional.1
  36.1 0.7 %copy.321 = f32[1,10,4096]{2,0,1:T(1,128)} copy(f32[1,10,4096]{2,0,1:T(1,128)S(1)} %get-tuple-element.3758) | data formatting | bytes 327680
  36.7 0.7 %copy.322 = f32[1,10,4096]{2,0,1:T(1,128)} copy(f32[1,10,4096]{2,0,1:T(1,128)S(1)} %get-tuple-element.3759) | data formatting | bytes 327680

commit v4 on v3

--- a/solution.py
+++ b/solution.py
@@ -211,6 +211,7 @@
 PICKED = 256
 SORTED = 1024
 CHUNK = 896
+TALL = CHUNK // 128
 DENSE = 1792
 NT = (((1,), (1,)), ((), ()))
 
@@ -437,7 +438,7 @@
 def whole_kernel(
     ids, obs_in, geo_in, frac_in, slot_in, corner_in, atlas_in, update, residual, flag,
     obs, geo, frac, slot, corner, atlas, picked, ordered, windows, landed, pixels, field,
-    across, down, slopes, seen_start, seen_first, gathered, near, far,
+    across, down, turned, stood, slopes, seen_start, seen_first, gathered, near, far,
     read_sems, send_window, recv_window, send_near, recv_near, send_far, recv_far,
 ):
     tex, me = lax.axis_index("tex"), lax.axis_index("view")
@@ -465,15 +466,32 @@
         read.wait()
     over, first, sizes = pack(ids, obs, geo, frac, slot, corner, picked, ordered)
     turns = jnp.where(first > 0.0, jnp.maximum(float(SORTED) - first, 0.0), 0.0).astype(jnp.int32)
-    back_by = lax.rem(senders - me, senders)
-    turns = pltpu.roll(turns, back_by, axis=0)
-    sizes = pltpu.roll(sizes, back_by, axis=0)
+    deep = math.isqrt(senders)
+    up, side = me // deep, lax.rem(me, deep)
     listed = ordered[...]
     pl.semaphore_wait(barrier, owners + senders - 2)
-    for step in range(1, senders):
-        windows[step] = folded(listed, turns[step, 0], sizes[step : step + 1, 0:1])
-        send(windows.at[step], landed, "view", step, send_window, recv_window)
-    landed[me] = folded(listed, turns[0, 0], sizes[0:1, 0:1])
+
+    def window_for(peer):
+        named = iota(turns.shape, 0) == peer
+        turn = jnp.sum(jnp.where(named, turns, 0)[:, 0:1])
+        size = jnp.sum(jnp.where(named, sizes, 0.0)[:, 0:1], axis=0, keepdims=True)
+        return folded(listed, turn, size)
+
+    apart = [(min(a, deep - a) + min(b, deep - b), a, b) for a in range(deep) for b in range(deep)]
+    for _, a, b in sorted(apart, reverse=True)[:-1]:
+        step = a * deep + b
+        peer = lax.rem(up + a, deep) * deep + lax.rem(side + b, deep)
+        windows[step] = window_for(peer)
+        pltpu.make_async_remote_copy(
+            src_ref=windows.at[step],
+            dst_ref=landed.at[me],
+            send_sem=send_window,
+            recv_sem=recv_window,
+            device_id=(tex, peer),
+            device_id_type=MESH,
+        ).start()
+    landed[me] = window_for(me)
+
 
     def hold(values):
         high, low = halves(values)
@@ -489,10 +507,14 @@
         seen = jnp.dot(field[...], across[c], preferred_element_type=F32)
         seen = seen.reshape(2, CHANNELS, BSIDE // 2, CHUNK) * rows
         seen = jnp.sum(seen[0] + seen[1], axis=1)
-        return [seen[k : k + 1] for k in range(CHANNELS)]
+        for j in range(TALL):
+            turned[:, j, :] = seen[:, j * 128 : j * 128 + 128]
+        return [turned[k] for k in range(CHANNELS)]
 
     def spread(c, rows, back):
-        back = jnp.concatenate(back, axis=0)
+        for k in range(CHANNELS):
+            turned[k] = back[k]
+        back = jnp.concatenate([turned[:, j, :] for j in range(TALL)], axis=1)
         terms = (back.reshape(1, CHANNELS, 1, CHUNK) * rows).reshape(2 * half_rows, CHUNK)
         high, low = halves(terms)
         columns = across[c, BSIDE : 3 * BSIDE, :]
@@ -525,6 +547,10 @@
         window = jnp.concatenate([window, jnp.zeros((ROWS, DENSE - WINDOW), F32)], axis=1)
         dense = dense + pltpu.roll(window, begins[j, 0], axis=1)
     pixels[...] = dense
+    for c in range(DENSE // CHUNK):
+        for j in range(TALL):
+            at = c * CHUNK + j * 128
+            stood[c, :, j, :] = dense[:, at : at + 128]
     count = jnp.sum(counts)
     over = jnp.maximum(over, jnp.where(count > DENSE, 1.0, 0.0))
     chunks = DENSE // CHUNK
@@ -546,10 +572,14 @@
         weight = jnp.where(used, weight, 0.0)
         down[c] = weight
         rows = weight.reshape(2, 1, BSIDE // 2, CHUNK)
-        factors, colors = optics(sample(c, rows), numbers[3:9])
+        standing = [stood[c, k] for k in range(9)]
+        factors, colors = optics(sample(c, rows), standing[3:9])
+        place = iota((TALL, 128), 0) * 128 + iota((TALL, 128), 1) + c * CHUNK
+        used = place.astype(F32) < count
         factors = [jnp.where(used, factor, 0.0) for factor in factors]
-        slopes[c] = jnp.concatenate(factors + [jnp.zeros((2, CHUNK), F32)], axis=0)
-        errors = [jnp.where(used, a - b, 0.0) for a, b in zip(colors, numbers[0:3])]
+        for k, factor in enumerate(factors):
+            slopes[c, k] = factor
+        errors = [jnp.where(used, a - b, 0.0) for a, b in zip(colors, standing[0:3])]
         spread(c, rows, pull(errors, factors))
         return carry
 
@@ -557,18 +587,17 @@
     start_now = -collected()
 
     def factors_of(c):
-        factors = slopes[c]
-        return [factors[k : k + 1] for k in range(14)]
+        return [slopes[c, k] for k in range(14)]
 
     def seen_of(c, kept):
         rows = down[c].reshape(2, 1, BSIDE // 2, CHUNK)
         colors = push(sample(c, rows), factors_of(c))
-        kept[c] = jnp.concatenate(colors + [jnp.zeros((5, CHUNK), F32)], axis=0)
+        for k in range(3):
+            kept[c, k] = colors[k]
 
     def spread_seen(c, kept):
         rows = down[c].reshape(2, 1, BSIDE // 2, CHUNK)
-        colors = kept[c]
-        spread(c, rows, pull([colors[k : k + 1] for k in range(3)], factors_of(c)))
+        spread(c, rows, pull([kept[c, k] for k in range(3)], factors_of(c)))
 
     def start_pass(c, carry):
         seen_of(c, seen_start)
@@ -647,6 +676,17 @@
     wait_all(far, send_far)
 
 
+def hand_on_kernel(update, residual, update_out, residual_out, sems):
+    copies = [
+        pltpu.make_async_copy(update, update_out, sems.at[0]),
+        pltpu.make_async_copy(residual, residual_out, sems.at[1]),
+    ]
+    for copy in copies:
+        copy.start()
+    for copy in copies:
+        copy.wait()
+
+
 def in_vmem(count):
     return [pl.BlockSpec(memory_space=pltpu.VMEM)] * count
 
@@ -677,9 +717,11 @@
             pltpu.VMEM((2 * half_rows, 256), BF16),
             pltpu.VMEM((DENSE // CHUNK, 4 * BSIDE, CHUNK), BF16),
             pltpu.VMEM((DENSE // CHUNK, BSIDE, CHUNK), F32),
-            pltpu.VMEM((DENSE // CHUNK, ROWS, CHUNK), F32),
-            pltpu.VMEM((DENSE // CHUNK, 8, CHUNK), F32),
-            pltpu.VMEM((DENSE // CHUNK, 8, CHUNK), F32),
+            pltpu.VMEM((CHANNELS, TALL, 128), F32),
+            pltpu.VMEM((DENSE // CHUNK, ROWS, TALL, 128), F32),
+            pltpu.VMEM((DENSE // CHUNK, 14, TALL, 128), F32),
+            pltpu.VMEM((DENSE // CHUNK, 3, TALL, 128), F32),
+            pltpu.VMEM((DENSE // CHUNK, 3, TALL, 128), F32),
             pltpu.VMEM((2 * half_rows, 128), F32),
             pltpu.VMEM((owners, 1, 128), F32),
             pltpu.VMEM((views, owners, 1, 128), F32),
@@ -700,7 +742,14 @@
     )
 
     def quick():
-        return update.reshape(texel_atlas.shape), residual.reshape(texel_atlas.shape)
+        handed = pl.pallas_call(
+            hand_on_kernel,
+            out_shape=(shaped((half_rows, 128), F32),) * 2,
+            in_specs=[pl.BlockSpec(memory_space=pl.ANY)] * 2,
+            out_specs=(pl.BlockSpec(memory_space=pl.ANY),) * 2,
+            scratch_shapes=[pltpu.SemaphoreType.DMA((2,))],
+        )(update, residual)
+        return tuple(part.reshape(texel_atlas.shape) for part in handed)
 
     def general():
         return general_step(

time: 37.6 us -> 36.5 us (0.971)
  local copies, waits for them, and re-layouts: 1.33 us -> 0 us
    unnamed x2 -> x0, local copies, waits for them, and re-layouts: 1.33 us -> none
    pallas_call x0 -> x1, Pallas kernels: none -> 0.74 us  [quick(): pl.pallas_call(hand_on_kernel, out_shape=(shaped((half_rows, 128), F32),)...]
    pallas_call x1, Pallas kernels: 34.5 us -> 33.9 us  [per_device(): pl.pallas_call(whole_kernel, out_shape=(shaped((half_rows, 128), F32),) *...]
where the time goes in v4:
time: 36.5 us; the launch traced here: 36.3 us
  Pallas kernels  34.6 us (95%)
  between operations  1.51 us (4%)
    pallas_call x1, Pallas kernels, per_device(): pl.pallas_call(whole_kernel, out_shape=(shaped((half_rows, 128), F32),) *...  33.9 us
    pallas_call x1, Pallas kernels, quick(): pl.pallas_call(hand_on_kernel, out_shape=(shaped((half_rows, 128), F32),)...  0.74 us

profile of v4, /device:TPU:0, one launch (start us, length us, event | category | flops | bytes accessed | tf_op | source)
XLA Modules:
  0.0 36.3 jit_solution(3841766526644375973)
XLA Ops:
  0.6 33.9 %shard_map.90 = (f32[320,128]{1,0:T(8,128)S(1)}, f32[320,128]{1,0:T(8,128)S(1)}, f32[1,128]{1,0:T(1,128)}) custom-call(s32[4,8]{1,0:T(4,128)} %bitcast.337, f32[3,8,768]{2,1,0:T(8,128)} %bitcast.336, f32[6,8,768]{2,1,0:T(8,128)} %bitcast.335, f32[8,2,768]{2,1,0:T(2,128)} %frac_in.1, s32[8,768]{1,0:T(8,128)} %slot_in.1, s32[8,768]{1,0:T(8,128)} %corner_in.1, ...), custom_call_target="tpu_custom_call" | custom-call | tf_op jit(solution)/shard_map/pallas_call | solution.py:700
  35.2 1.0 %conditional.1 = (f32[1,10,4096]{2,0,1:T(1,128)}, f32[1,10,4096]{2,0,1:T(1,128)}) conditional(s32[]{:T(128)} %bitcast.101, (f32[320,128]{1,0:T(8,128)S(1)}, f32[320,128]{1,0:T(8,128)S(1)}) %tuple.517, (s32[8,1,4]{0,2,1:T(4,128)}, s32[8,768]{1,0:T(8,128)}, s32[8,768]{1,0:T(8,128)}, f32[8,2,768]{2,1,0:T(2,128)}, f32[1,10,4096]{2,0,1:T(1,128)}, ...), branch_computations={%region_0.0_spmd, %region_1.73_spmd} | conditional | flops 74039418880 | bytes 262689136 | solution.py:759
  35.2 0.7 %branch_0_fun.1 = (f32[320,128]{1,0:T(8,128)}, f32[320,128]{1,0:T(8,128)}) custom-call(f32[320,128]{1,0:T(8,128)S(1)} %get-tuple-element.2254.update, f32[320,128]{1,0:T(8,128)S(1)} %get-tuple-element.2255.residual), custom_call_target="tpu_custom_call" | custom-call | tf_op jit(solution)/shard_map/cond/branch_0_fun/pallas_call | solution.py:745

commit v5 on v4

--- a/solution.py
+++ b/solution.py
@@ -508,13 +508,13 @@
         seen = seen.reshape(2, CHANNELS, BSIDE // 2, CHUNK) * rows
         seen = jnp.sum(seen[0] + seen[1], axis=1)
         for j in range(TALL):
-            turned[:, j, :] = seen[:, j * 128 : j * 128 + 128]
-        return [turned[k] for k in range(CHANNELS)]
+            turned[2 * c, :, j, :] = seen[:, j * 128 : j * 128 + 128]
+        return [turned[2 * c, k] for k in range(CHANNELS)]
 
     def spread(c, rows, back):
         for k in range(CHANNELS):
-            turned[k] = back[k]
-        back = jnp.concatenate([turned[:, j, :] for j in range(TALL)], axis=1)
+            turned[2 * c + 1, k] = back[k]
+        back = jnp.concatenate([turned[2 * c + 1, :, j, :] for j in range(TALL)], axis=1)
         terms = (back.reshape(1, CHANNELS, 1, CHUNK) * rows).reshape(2 * half_rows, CHUNK)
         high, low = halves(terms)
         columns = across[c, BSIDE : 3 * BSIDE, :]
@@ -555,8 +555,8 @@
     over = jnp.maximum(over, jnp.where(count > DENSE, 1.0, 0.0))
     chunks = DENSE // CHUNK
 
-    def first_pass(c, carry):
-        numbers = pixels[:, pl.ds(pl.multiple_of(c * CHUNK, CHUNK), CHUNK)]
+    def first_pass(c):
+        numbers = pixels[:, c * CHUNK : c * CHUNK + CHUNK]
         numbers = [numbers[k : k + 1] for k in range(ROWS)]
         used = (iota((1, CHUNK), 1) + c * CHUNK).astype(F32) < count
         frac_x, frac_y, spot = numbers[9:12]
@@ -581,9 +581,9 @@
             slopes[c, k] = factor
         errors = [jnp.where(used, a - b, 0.0) for a, b in zip(colors, standing[0:3])]
         spread(c, rows, pull(errors, factors))
-        return carry
-
-    lax.fori_loop(0, chunks, first_pass, 0)
+
+    for c in range(chunks):
+        first_pass(c)
     start_now = -collected()
 
     def factors_of(c):
@@ -599,22 +599,22 @@
         rows = down[c].reshape(2, 1, BSIDE // 2, CHUNK)
         spread(c, rows, pull([kept[c, k] for k in range(3)], factors_of(c)))
 
-    def start_pass(c, carry):
+    def start_pass(c):
         seen_of(c, seen_start)
         spread_seen(c, seen_start)
-        return carry
-
-    def first_seen(c, carry):
+
+    def first_seen(c):
         seen_of(c, seen_first)
-        return carry
 
     hold(start_now)
     gathered[...] = jnp.zeros(gathered.shape, F32)
-    lax.fori_loop(0, chunks, start_pass, 0)
+    for c in range(chunks):
+        start_pass(c)
     first_now = collected() + DAMPING * start_now
     hold(first_now)
     gathered[...] = jnp.zeros(gathered.shape, F32)
-    lax.fori_loop(0, chunks, first_seen, 0)
+    for c in range(chunks):
+        first_seen(c)
 
     start_start = jnp.sum(start_now * start_now)
     start_first = jnp.sum(start_now * first_now)
@@ -717,7 +717,7 @@
             pltpu.VMEM((2 * half_rows, 256), BF16),
             pltpu.VMEM((DENSE // CHUNK, 4 * BSIDE, CHUNK), BF16),
             pltpu.VMEM((DENSE // CHUNK, BSIDE, CHUNK), F32),
-            pltpu.VMEM((CHANNELS, TALL, 128), F32),
+            pltpu.VMEM((2 * DENSE // CHUNK, CHANNELS, TALL, 128), F32),
             pltpu.VMEM((DENSE // CHUNK, ROWS, TALL, 128), F32),
             pltpu.VMEM((DENSE // CHUNK, 14, TALL, 128), F32),
             pltpu.VMEM((DENSE // CHUNK, 3, TALL, 128), F32),

time: 36.5 us -> 35.6 us (0.975)
  Pallas kernels: 34.6 us -> 33.7 us
    pallas_call x1, Pallas kernels: 33.9 us -> 32.9 us  [per_device(): pl.pallas_call(whole_kernel, out_shape=(shaped((half_rows, 128), F32),) *...]
where the time goes in v5:
time: 35.6 us; the launch traced here: 35.4 us
  Pallas kernels  33.7 us (95%)
  between operations  1.51 us (4%)
    pallas_call x1, Pallas kernels, per_device(): pl.pallas_call(whole_kernel, out_shape=(shaped((half_rows, 128), F32),) *...  32.9 us
    pallas_call x1, Pallas kernels, quick(): pl.pallas_call(hand_on_kernel, out_shape=(shaped((half_rows, 128), F32),)...  0.74 us

profile of v5, /device:TPU:0, one launch (start us, length us, event | category | flops | bytes accessed | tf_op | source)
XLA Modules:
  0.0 35.4 jit_solution(1196791151509145277)
XLA Ops:
  0.6 32.9 %shard_map.90 = (f32[320,128]{1,0:T(8,128)S(1)}, f32[320,128]{1,0:T(8,128)S(1)}, f32[1,128]{1,0:T(1,128)}) custom-call(s32[4,8]{1,0:T(4,128)} %bitcast.337, f32[3,8,768]{2,1,0:T(8,128)} %bitcast.336, f32[6,8,768]{2,1,0:T(8,128)} %bitcast.335, f32[8,2,768]{2,1,0:T(2,128)} %frac_in.1, s32[8,768]{1,0:T(8,128)} %slot_in.1, s32[8,768]{1,0:T(8,128)} %corner_in.1, ...), custom_call_target="tpu_custom_call" | custom-call | tf_op jit(solution)/shard_map/pallas_call | solution.py:700
  34.3 1.0 %conditional.1 = (f32[1,10,4096]{2,0,1:T(1,128)}, f32[1,10,4096]{2,0,1:T(1,128)}) conditional(s32[]{:T(128)} %bitcast.101, (f32[320,128]{1,0:T(8,128)S(1)}, f32[320,128]{1,0:T(8,128)S(1)}) %tuple.517, (s32[8,1,4]{0,2,1:T(4,128)}, s32[8,768]{1,0:T(8,128)}, s32[8,768]{1,0:T(8,128)}, f32[8,2,768]{2,1,0:T(2,128)}, f32[1,10,4096]{2,0,1:T(1,128)}, ...), branch_computations={%region_0.0_spmd, %region_1.73_spmd} | conditional | flops 74039418880 | bytes 262689136 | solution.py:759
  34.3 0.7 %branch_0_fun.1 = (f32[320,128]{1,0:T(8,128)}, f32[320,128]{1,0:T(8,128)}) custom-call(f32[320,128]{1,0:T(8,128)S(1)} %get-tuple-element.2254.update, f32[320,128]{1,0:T(8,128)S(1)} %get-tuple-element.2255.residual), custom_call_target="tpu_custom_call" | custom-call | tf_op jit(solution)/shard_map/cond/branch_0_fun/pallas_call | solution.py:745

commit v6 on v5

--- a/solution.py
+++ b/solution.py
@@ -331,18 +331,24 @@
     return jnp.concatenate([window[:, :WINDOW], jnp.concatenate(low, axis=1)], axis=0)
 
 
+def far_first(me, count):
+    deep = math.isqrt(count)
+    apart = [(min(a, deep - a) + min(b, deep - b), a, b) for a in range(deep) for b in range(deep)]
+    up, side = me // deep, lax.rem(me, deep)
+    for _, a, b in sorted(apart, reverse=True)[:-1]:
+        yield a * deep + b, lax.rem(up + a, deep) * deep + lax.rem(side + b, deep)
+
+
 def greet(barrier, tex, view, owners, views):
-    for step in range(1, views):
-        peer = lax.rem(view + step, views)
+    for _, peer in far_first(view, views):
         pl.semaphore_signal(barrier, inc=1, device_id=(tex, peer), device_id_type=MESH)
     for step in range(1, owners):
         peer = lax.rem(tex + step, owners)
         pl.semaphore_signal(barrier, inc=1, device_id=(peer, view), device_id_type=MESH)
 
 
-def send(source, target, axis, step, send_sem, recv_sem):
-    count, me = lax.axis_size(axis), lax.axis_index(axis)
-    peer = lax.rem(me + step, count)
+def send(source, target, axis, peer, send_sem, recv_sem):
+    me = lax.axis_index(axis)
     pltpu.make_async_remote_copy(
         src_ref=source,
         dst_ref=target.at[me],
@@ -466,8 +472,6 @@
         read.wait()
     over, first, sizes = pack(ids, obs, geo, frac, slot, corner, picked, ordered)
     turns = jnp.where(first > 0.0, jnp.maximum(float(SORTED) - first, 0.0), 0.0).astype(jnp.int32)
-    deep = math.isqrt(senders)
-    up, side = me // deep, lax.rem(me, deep)
     listed = ordered[...]
     pl.semaphore_wait(barrier, owners + senders - 2)
 
@@ -477,19 +481,9 @@
         size = jnp.sum(jnp.where(named, sizes, 0.0)[:, 0:1], axis=0, keepdims=True)
         return folded(listed, turn, size)
 
-    apart = [(min(a, deep - a) + min(b, deep - b), a, b) for a in range(deep) for b in range(deep)]
-    for _, a, b in sorted(apart, reverse=True)[:-1]:
-        step = a * deep + b
-        peer = lax.rem(up + a, deep) * deep + lax.rem(side + b, deep)
+    for step, peer in far_first(me, senders):
         windows[step] = window_for(peer)
-        pltpu.make_async_remote_copy(
-            src_ref=windows.at[step],
-            dst_ref=landed.at[me],
-            send_sem=send_window,
-            recv_sem=recv_window,
-            device_id=(tex, peer),
-            device_id_type=MESH,
-        ).start()
+        send(windows.at[step], landed, "view", peer, send_window, recv_window)
     landed[me] = window_for(me)
 
 
@@ -642,12 +636,12 @@
         line = jnp.where(place == k, value, line)
     near[tex] = line
     for step in range(1, owners):
-        send(near.at[tex], near, "tex", step, send_near, recv_near)
+        send(near.at[tex], near, "tex", lax.rem(tex + step, owners), send_near, recv_near)
     spread_seen(0, seen_first)
     wait_all(near, recv_near)
     far[me] = near[...]
-    for step in range(1, senders):
-        send(near, far, "view", step, send_far, recv_far)
+    for _, peer in far_first(me, senders):
+        send(near, far, "view", peer, send_far, recv_far)
     for c in range(1, chunks):
         spread_seen(c, seen_first)
     second_now = collected() + DAMPING * first_now

time: 35.6 us -> 35.6 us (level)
  no operation moved by 1% of the time
where the time goes in v6:
time: 35.6 us; the launch traced here: 35.3 us
  Pallas kernels  33.5 us (94%)
  between operations  1.51 us (4%)
    pallas_call x1, Pallas kernels, per_device(): pl.pallas_call(whole_kernel, out_shape=(shaped((half_rows, 128), F32),) *...  32.8 us
    pallas_call x1, Pallas kernels, quick(): pl.pallas_call(hand_on_kernel, out_shape=(shaped((half_rows, 128), F32),)...  0.74 us

profile of v6, /device:TPU:0, one launch (start us, length us, event | category | flops | bytes accessed | tf_op | source)
XLA Modules:
  0.0 35.3 jit_solution(16639875938496619480)
XLA Ops:
  0.6 32.8 %shard_map.90 = (f32[320,128]{1,0:T(8,128)S(1)}, f32[320,128]{1,0:T(8,128)S(1)}, f32[1,128]{1,0:T(1,128)}) custom-call(s32[4,8]{1,0:T(4,128)} %bitcast.337, f32[3,8,768]{2,1,0:T(8,128)} %bitcast.336, f32[6,8,768]{2,1,0:T(8,128)} %bitcast.335, f32[8,2,768]{2,1,0:T(2,128)} %frac_in.1, s32[8,768]{1,0:T(8,128)} %slot_in.1, s32[8,768]{1,0:T(8,128)} %corner_in.1, ...), custom_call_target="tpu_custom_call" | custom-call | tf_op jit(solution)/shard_map/pallas_call | solution.py:694
  34.1 1.0 %conditional.1 = (f32[1,10,4096]{2,0,1:T(1,128)}, f32[1,10,4096]{2,0,1:T(1,128)}) conditional(s32[]{:T(128)} %bitcast.101, (f32[320,128]{1,0:T(8,128)S(1)}, f32[320,128]{1,0:T(8,128)S(1)}) %tuple.517, (s32[8,1,4]{0,2,1:T(4,128)}, s32[8,768]{1,0:T(8,128)}, s32[8,768]{1,0:T(8,128)}, f32[8,2,768]{2,1,0:T(2,128)}, f32[1,10,4096]{2,0,1:T(1,128)}, ...), branch_computations={%region_0.0_spmd, %region_1.73_spmd} | conditional | flops 74039418880 | bytes 262689136 | solution.py:753
  34.1 0.7 %branch_0_fun.1 = (f32[320,128]{1,0:T(8,128)}, f32[320,128]{1,0:T(8,128)}) custom-call(f32[320,128]{1,0:T(8,128)S(1)} %get-tuple-element.2254.update, f32[320,128]{1,0:T(8,128)S(1)} %get-tuple-element.2255.residual), custom_call_target="tpu_custom_call" | custom-call | tf_op jit(solution)/shard_map/cond/branch_0_fun/pallas_call | solution.py:739
